TPU v7x, 128 devices: a whole 4x4x4 slice. The times are simulated.
128 devices in a mesh: grp: 4 (over z), elem: 32 (over x, y, core).
Axes of the slice: x: 4, y: 4, z: 4, core: 2. Of those that a mesh axis runs over, the one named last changes fastest.
Arguments:
- velocity: float32 [3, 343, 16384], P(None, None, ('grp', 'elem')), may hold values from -0.6 to 0.6
- adjoint: float32 [3, 343, 16384], P(None, None, ('grp', 'elem')), may hold values from -0.6 to 0.6
- spacing: float32 [3, 16384], P(None, ('grp', 'elem')), may hold values from 0.5 to 2
- elem_count: int32 [128], P(('grp', 'elem')), may hold values from 32 to 128, as said below
- design_map: int32 [8, 16384], P(None, ('grp', 'elem')), may hold values from 0 to 262143, as said below
Outputs:
- direction: float32 [3, 262144], P(None, ('grp', 'elem'))
- objective: float32 [], replicated
Inputs may be any that keep to these rules, and one draw needn't show every extreme that they name: `elem_count`: the largest count equals 128 in every draw. `design_map`: design node d belongs to the device numbered d // 2048, counting grp first and elem second. Every entry of a device's columns names a node of a device whose elem index differs from that device's by at most one, cyclically over the elem axis, in any group.
All inputs are finite; a program needn't handle non-finite values.
Results may differ from a plain program's by a relative error of at most 0.0003.
Values sent between devices are 32-bit elements; how exact they have to be, the bound alone decides.
No kernel may reach another device: no remote copies, remote signals or barrier semaphores. Data moves between devices by JAX's collectives and lax.ppermute only.
A program may use at most 64 MiB of HBM per device.

v0:
```python
import functools

import jax
import jax.numpy as jnp
import numpy as np
from jax import lax
from jax.sharding import Mesh
from jax.sharding import PartitionSpec as P

P_SIZE = 7
ND_DEV = 2048
ELEM = ("elem_0", "elem_1", "elem_2")
GRP_ELEM = ("grp", "elem_0", "elem_1", "elem_2")


def in_blocks(array, dim, devices):
    lengths = array.shape
    parts = array.reshape(*lengths[:dim], devices, lengths[dim] // devices, *lengths[dim + 1 :])
    return jnp.moveaxis(parts, dim, 0)


def sent_and_summed(array, axis, dim):
    parts = in_blocks(array, dim, lax.axis_size(axis))
    arrived = lax.all_to_all(parts, axis, split_axis=0, concat_axis=0, tiled=True)
    return arrived.sum(axis=0)


def passed_along(array, axis, by):
    devices = lax.axis_size(axis)
    return lax.ppermute(array, axis, [(i, (i + by) % devices) for i in range(devices)])


def by_axis(array, axes):
    return functools.reduce(lax.psum, axes, array)


def lobatto(degree):
    points = np.cos(np.pi * np.arange(degree + 1) / degree)
    for sweep in range(60):
        lower = np.ones(degree + 1)
        upper = points.copy()
        for order in range(2, degree + 1):
            lower, upper = (upper, ((2 * order - 1) * points * upper - (order - 1) * lower) / order)
        points = points - (points * upper - lower) / ((degree + 1) * upper)
    lower = np.ones(degree + 1)
    upper = points.copy()
    for order in range(2, degree + 1):
        lower, upper = (upper, ((2 * order - 1) * points * upper - (order - 1) * lower) / order)
    return (points[::-1].copy(), upper[::-1].copy())


def tables():
    degree = P_SIZE - 1
    points, values = lobatto(degree)
    weights = 2.0 / (degree * (degree + 1) * values**2)
    derivative = np.zeros((P_SIZE, P_SIZE))
    for i in range(P_SIZE):
        for j in range(P_SIZE):
            if i != j:
                derivative[i, j] = values[i] / (values[j] * (points[i] - points[j]))
    derivative[0, 0] = -degree * (degree + 1) / 4.0
    derivative[P_SIZE - 1, P_SIZE - 1] = degree * (degree + 1) / 4.0
    coords = np.meshgrid(points, points, points, indexing="ij")
    coords = [c.reshape(-1) for c in coords]
    spread = np.meshgrid(weights, weights, weights, indexing="ij")
    quadrature = (spread[0] * spread[1] * spread[2]).reshape(-1)
    vertex_grad = np.zeros((3, 8, P_SIZE**3))
    for vertex in range(8):
        signs = [2.0 * (vertex >> 2 - m & 1) - 1.0 for m in range(3)]
        factors = [(1.0 + signs[m] * coords[m]) / 2.0 for m in range(3)]
        for j in range(3):
            others = [factors[m] for m in range(3) if m != j]
            vertex_grad[j, vertex] = signs[j] / 2.0 * others[0] * others[1] * quadrature
    unit = np.eye(P_SIZE)
    directional = np.stack(
        [
            np.kron(np.kron(derivative, unit), unit),
            np.kron(np.kron(unit, derivative), unit),
            np.kron(np.kron(unit, unit), derivative),
        ]
    )
    return (
        jnp.asarray(directional, jnp.float32),
        jnp.asarray(vertex_grad, jnp.float32),
        jnp.asarray(quadrature, jnp.float32),
    )


def element_terms(velocity, adjoint, spacing, directional, vertex_grad, quadrature):
    factor = 2.0 / spacing
    jacobian = spacing[0] * spacing[1] * spacing[2] / 8.0
    highest = lax.Precision.HIGHEST

    def gradient(field):
        return [
            [
                jnp.dot(directional[j], field[i], precision=highest) * factor[j][None, :]
                for j in range(3)
            ]
            for i in range(3)
        ]

    grad_u = gradient(velocity)
    grad_w = gradient(adjoint)
    inner = grad_u[0][0] * grad_w[0][0]
    squared = grad_u[0][0] * grad_u[0][0]
    for i in range(3):
        for k in range(3):
            if i + k > 0:
                inner = inner + grad_u[i][k] * grad_w[i][k]
                squared = squared + grad_u[i][k] * grad_u[i][k]
    cross = [
        [
            grad_u[0][c] * grad_w[0][j] + grad_u[1][c] * grad_w[1][j] + grad_u[2][c] * grad_w[2][j]
            for j in range(3)
        ]
        for c in range(3)
    ]
    rows = []
    for c in range(3):
        total = None
        for j in range(3):
            stress = -cross[c][j] - cross[j][c]
            if c == j:
                stress = stress + inner
            piece = jnp.dot(vertex_grad[j], stress, precision=highest) * factor[j][None, :]
            total = piece if total is None else total + piece
        rows.append(total * jacobian[None, :])
    terms = jnp.stack(rows)
    dissipated = jacobian * jnp.dot(quadrature, squared, precision=highest)
    return (terms, dissipated)


def body(velocity, adjoint, spacing, elem_count, design_map):
    slots = velocity.shape[-1]
    block = min(256, slots)
    groups = lax.axis_size("grp")
    columns = lax.axis_size(ELEM)
    design_total = ND_DEV * groups * columns
    directional, vertex_grad, quadrature = tables()
    extent = 3 * groups * ND_DEV
    home_col = lax.axis_index(ELEM)
    owner = design_map // ND_DEV
    offset = (owner % columns - home_col + 1 + columns) % columns
    target = (offset * groups + owner // columns) * ND_DEV + design_map % ND_DEV
    count = elem_count[0]
    live_blocks = (count + block - 1) // block

    def step(index, carry):
        assembled, spent = carry
        start = index * block
        terms, dissipated = element_terms(
            velocity, adjoint, spacing, directional, vertex_grad, quadrature
        )
        live = (start + jnp.arange(block, dtype=jnp.int32) < count).astype(jnp.float32)
        terms = terms * live[None, None, :]
        assembled = assembled.at[:, target.reshape(-1)].add(terms.reshape(3, -1))
        return (assembled, spent + jnp.sum(dissipated * live))

    init = (jnp.zeros((3, extent), jnp.float32), jnp.zeros((), jnp.float32))
    assembled, spent = lax.fori_loop(0, live_blocks, step, init)
    layered = assembled.reshape(3, 3, groups, ND_DEV)
    nearby = sent_and_summed(layered, "grp", 2).reshape(3, 3, ND_DEV)
    from_above = passed_along(nearby[:, 0], ELEM, -1)
    from_below = passed_along(nearby[:, 2], ELEM, 1)
    gradient_sum = nearby[:, 1] + from_above + from_below
    squares = jnp.sum(gradient_sum * gradient_sum)
    spent_total, square_total = (by_axis(spent, GRP_ELEM), by_axis(squares, GRP_ELEM))
    direction = gradient_sum * lax.rsqrt(square_total / (3.0 * design_total) + 1e-06)
    objective = spent_total / (P_SIZE**3 * slots * groups * columns)
    return (direction, objective)


def solution(mesh):
    finer = Mesh(
        mesh.devices.reshape(mesh.shape["grp"], 4, 4, 2), ("grp", "elem_0", "elem_1", "elem_2")
    )
    in_specs = (
        P(None, None, GRP_ELEM),
        P(None, None, GRP_ELEM),
        P(None, GRP_ELEM),
        P(GRP_ELEM),
        P(None, GRP_ELEM),
    )
    out_specs = (P(None, GRP_ELEM), P())
    return jax.shard_map(body, mesh=finer, in_specs=in_specs, out_specs=out_specs, check_vma=False)
```

profile of v0, /device:TPU:1, one launch (start us, length us, event | category | flops | bytes accessed | tf_op | source)
XLA Modules:
  0.0 128.9 jit_solution(7839216677726242241)
XLA Ops:
  1.4 0.8 fusion.137
  2.2 0.8 slice_multiply_fusion
  3.0 0.7 broadcast_divide_fusion.1
  3.7 1.8 %convolution_multiply_fusion.15 = f32[343,128]{1,0:T(8,128)S(1)} fusion(f32[343,343]{1,0:T(8,128)} %constant.163, f32[3,343,128]{2,1,0:T(8,128)} %param.10, f32[128]{0:T(128)S(1)} %get-tuple-element.476), kind=kOutput, calls=%fused_computation.32 | convolution fusion | flops 180752768 | bytes 880640 | tf_op jit(solution)/shard_map/while/body/dot_general | solution.py:97
  5.5 1.8 %convolution_multiply_fusion.13 = f32[343,128]{1,0:T(8,128)S(1)} fusion(f32[343,343]{1,0:T(8,128)} %constant.163, f32[3,343,128]{2,1,0:T(8,128)} %param.10, f32[128]{0:T(128)S(1)} %get-tuple-element.476), kind=kOutput, calls=%fused_computation.30 | convolution fusion | flops 180752768 | bytes 880640 | tf_op jit(solution)/shard_map/while/body/dot_general | solution.py:97
  7.3 1.8 %convolution_multiply_fusion.17 = f32[343,128]{1,0:T(8,128)S(1)} fusion(f32[343,343]{1,0:T(8,128)} %constant.163, f32[3,343,128]{2,1,0:T(8,128)} %param.10, f32[128]{0:T(128)S(1)} %get-tuple-element.476), kind=kOutput, calls=%fused_computation.34 | convolution fusion | flops 180752768 | bytes 880640 | tf_op jit(solution)/shard_map/while/body/dot_general | solution.py:97
  9.1 1.8 %convolution_multiply_fusion.5 = f32[343,128]{1,0:T(8,128)S(1)} fusion(f32[343,343]{1,0:T(8,128)} %constant.167, f32[3,343,128]{2,1,0:T(8,128)} %param.10, f32[128]{0:T(128)S(1)} %get-tuple-element.477), kind=kOutput, calls=%fused_computation.22 | convolution fusion | flops 180752768 | bytes 880640 | tf_op jit(solution)/shard_map/while/body/dot_general | solution.py:97
  10.9 1.8 %convolution_multiply_fusion.1 = f32[343,128]{1,0:T(8,128)S(1)} fusion(f32[343,343]{1,0:T(8,128)} %constant.167, f32[3,343,128]{2,1,0:T(8,128)} %param.10, f32[128]{0:T(128)S(1)} %get-tuple-element.477), kind=kOutput, calls=%fused_computation.18 | convolution fusion | flops 180752768 | bytes 880640 | tf_op jit(solution)/shard_map/while/body/dot_general | solution.py:97
  12.7 1.8 %convolution_multiply_fusion.9 = f32[343,128]{1,0:T(8,128)S(1)} fusion(f32[343,343]{1,0:T(8,128)} %constant.167, f32[3,343,128]{2,1,0:T(8,128)} %param.10, f32[128]{0:T(128)S(1)} %get-tuple-element.477), kind=kOutput, calls=%fused_computation.26 | convolution fusion | flops 180752768 | bytes 880640 | tf_op jit(solution)/shard_map/while/body/dot_general | solution.py:97
  14.4 1.8 %convolution_multiply_fusion.7 = f32[343,128]{1,0:T(8,128)S(1)} fusion(f32[343,343]{1,0:T(8,128)} %constant.165, f32[3,343,128]{2,1,0:T(8,128)} %param.10, f32[128]{0:T(128)S(1)} %get-tuple-element.478), kind=kOutput, calls=%fused_computation.24 | convolution fusion | flops 180752768 | bytes 880640 | tf_op jit(solution)/shard_map/while/body/dot_general | solution.py:97
  16.2 1.8 %convolution_multiply_fusion.11 = f32[343,128]{1,0:T(8,128)S(1)} fusion(f32[343,343]{1,0:T(8,128)} %constant.165, f32[3,343,128]{2,1,0:T(8,128)} %param.10, f32[128]{0:T(128)S(1)} %get-tuple-element.478), kind=kOutput, calls=%fused_computation.28 | convolution fusion | flops 180752768 | bytes 880640 | tf_op jit(solution)/shard_map/while/body/dot_general | solution.py:97
  18.0 1.8 %convolution_multiply_fusion.16 = f32[343,128]{1,0:T(8,128)S(1)} fusion(f32[343,343]{1,0:T(8,128)} %constant.163, f32[3,343,128]{2,1,0:T(8,128)} %param.11, f32[128]{0:T(128)S(1)} %get-tuple-element.476), kind=kOutput, calls=%fused_computation.33 | convolution fusion | flops 180752768 | bytes 880640 | tf_op jit(solution)/shard_map/while/body/dot_general | solution.py:97
  19.8 1.8 %convolution_multiply_fusion.14 = f32[343,128]{1,0:T(8,128)S(1)} fusion(f32[343,343]{1,0:T(8,128)} %constant.163, f32[3,343,128]{2,1,0:T(8,128)} %param.11, f32[128]{0:T(128)S(1)} %get-tuple-element.476), kind=kOutput, calls=%fused_computation.31 | convolution fusion | flops 180752768 | bytes 880640 | tf_op jit(solution)/shard_map/while/body/dot_general | solution.py:97
  21.6 1.8 %convolution_multiply_fusion.12 = f32[343,128]{1,0:T(8,128)S(1)} fusion(f32[343,343]{1,0:T(8,128)} %constant.163, f32[3,343,128]{2,1,0:T(8,128)} %param.11, f32[128]{0:T(128)S(1)} %get-tuple-element.476), kind=kOutput, calls=%fused_computation.29 | convolution fusion | flops 180752768 | bytes 880640 | tf_op jit(solution)/shard_map/while/body/dot_general | solution.py:97
  23.4 1.8 %convolution_multiply_fusion.8 = f32[343,128]{1,0:T(8,128)S(1)} fusion(f32[343,343]{1,0:T(8,128)} %constant.167, f32[3,343,128]{2,1,0:T(8,128)} %param.11, f32[128]{0:T(128)S(1)} %get-tuple-element.477), kind=kOutput, calls=%fused_computation.25 | convolution fusion | flops 180752768 | bytes 880640 | tf_op jit(solution)/shard_map/while/body/dot_general | solution.py:97
  25.2 1.8 %convolution_multiply_fusion.4 = f32[343,128]{1,0:T(8,128)S(1)} fusion(f32[343,343]{1,0:T(8,128)} %constant.167, f32[3,343,128]{2,1,0:T(8,128)} %param.11, f32[128]{0:T(128)S(1)} %get-tuple-element.477), kind=kOutput, calls=%fused_computation.21 | convolution fusion | flops 180752768 | bytes 880640 | tf_op jit(solution)/shard_map/while/body/dot_general | solution.py:97
  26.9 1.8 %convolution_multiply_fusion = f32[343,128]{1,0:T(8,128)S(1)} fusion(f32[343,343]{1,0:T(8,128)} %constant.167, f32[3,343,128]{2,1,0:T(8,128)} %param.11, f32[128]{0:T(128)S(1)} %get-tuple-element.477), kind=kOutput, calls=%fused_computation.17 | convolution fusion | flops 180752768 | bytes 880640 | tf_op jit(solution)/shard_map/while/body/dot_general | solution.py:97
  28.7 1.6 %convolution_multiply_fusion.10 = f32[343,128]{1,0:T(8,128)S(1)} fusion(f32[343,343]{1,0:T(8,128)S(1)} %copy-done, f32[3,343,128]{2,1,0:T(8,128)} %param.11, f32[128]{0:T(128)S(1)} %get-tuple-element.478), kind=kOutput, calls=%fused_computation.27 | convolution fusion | flops 180752768 | bytes 822852 | tf_op jit(solution)/shard_map/while/body/dot_general | solution.py:97
  30.4 0.7 convolution_multiply_fusion.6
  31.1 0.9 convolution_multiply_fusion.2
  32.0 1.8 %multiply_add_fusion.1 = (f32[343,128]{1,0:T(8,128)S(1)}, f32[343,128]{1,0:T(8,128)S(1)}, f32[343,128]{1,0:T(8,128)S(1)}, f32[343,128]{1,0:T(8,128)S(1)}, f32[34...) fusion(f32[343,128]{1,0:T(8,128)S(1)} %convolution_multiply_fusion, ...), kind=kOutput, calls=%fused_computation.96 | convolution fusion | flops 182816256 | bytes 5037636 | tf_op jit(solution)/shard_map/while/body/dot_general | solution.py:97
  36.2 0.3 convolution_bitcast_fusion
  36.6 4.8 %broadcast_in_dim.2 = f32[3,24576]{0,1:T(8,128)} broadcast(f32[]{:T(128)} %constant.137.clone.1), dimensions={} | broadcast | bytes 294916 | tf_op jit(solution)/shard_map/broadcast_in_dim | solution.py:160
  41.5 17.5 %while.16 = (s32[]{:T(128)}, f32[3,24576]{0,1:T(8,128)}, f32[]{:T(128)}, s32[]{:T(128)}, s32[8,128]{1,0:T(8,128)S(1)}, /*index=5*/f32[3,128]{1,0:T(4,128)S(1)}, ...) while((s32[]{:T(128)}, f32[3,24576]{0,1:T(8,128)}, ...), condition=%wide.region_3.4_spmd, body=%wide.region_0.3_spmd.sunk | while | flops 35459 | bytes 167145 | solution.py:161
  41.5 1.3 %fusion.141 = f32[]{:T(128)} fusion(f32[128]{0:T(128)S(1)} %get-tuple-element.670, f32[128]{0:T(128)S(1)} %get-tuple-element.669, s32[]{:T(128)} %get-tuple-element.668, s32[]{:T(128)S(6)} %mul.1015), kind=kLoop, calls=%fused_computation.11.clone.1 | loop fusion | flops 767 | bytes 1036 | tf_op jit(solution)/shard_map/while/body/reduce_sum | solution.py:158
  43.4 0.7 compare_convert_fusion.2
  44.4 14.6 %scatter_fusion = f32[3,24576]{0,1:T(8,128)} fusion(f32[3,24576]{0,1:T(8,128)} %get-tuple-element.632, s32[1024]{0:T(1024)S(1)} %bitcast.139, f32[1024,3]{1,0:T(8,128)S(1)} %copy.36), kind=kCustom, calls=%fused_computation.clone.1 | custom fusion | flops 3072 | bytes 40960 | tf_op jit(solution)/shard_map/while/body/scatter-add | solution.py:157
  59.0 7.6 %copy.30 = f32[3,3,4,1,2048]{4,2,1,0,3:T(4,128)S(1)} copy(f32[3,3,4,1,2048]{0,4,2,1,3:T(8,128)} %bitcast.135) | data formatting | bytes 589824 | tf_op jit(solution)/shard_map/reshape;reshape | solution.py:18
  66.9 11.4 %all_to_all.5 = f32[4,3,3,1,2048]{4,3,2,1,0:T(1,128)S(1)} all-to-all(f32[4,3,3,1,2048]{4,3,2,1,0:T(1,128)S(1)} %copy.23), channel_id=1, replica_groups=mesh['grp'=4,'elem_0'=4,'elem_1'=4,'elem_2'=2] {'grp'}, dimensions={0} | all-to-all | bytes 589824 | tf_op jit(solution)/shard_map/all_to_all | solution.py:24
  78.4 0.3 reduce_sum.31
  78.8 0.4 copy.33
  79.2 0.3 copy.25
  79.5 2.2 %collective-permute-start = (f32[3,2048]{1,0:T(4,128)S(1)}, f32[3,2048]{1,0:T(4,128)S(1)}, u32[]{:S(2)}, u32[]{:S(2)}) collective-permute-start(f32[3,2048]{1,0:T(4,128)S(1)} %copy.25), channel_id=1, source_target_pairs={{0,31},{1,0},{2,1},{3,2},{4,3},{5,4},{6,5},{7,6},{8,7},{9,8},{10,9... | collective-permute-start | bytes 73736 | tf_op jit(solution)/shard_map/ppermute | solution.py:30
  81.7 0.4 copy.34
  82.1 0.3 copy.27
  82.4 1.2 collective-permute-start.1
  83.6 0.4 copy.32
  84.0 0.5 collective-permute-done
  84.5 0.4 copy.26
  84.9 1.5 %collective-permute-done.1 = f32[3,2048]{1,0:T(4,128)S(1)} collective-permute-done((f32[3,2048]{1,0:T(4,128)S(1)}, f32[3,2048]{1,0:T(4,128)S(1)}, u32[]{:S(2)}, u32[]{:S(2)}) %collective-permute-start.1) | collective-permute-done | bytes 24608 | tf_op jit(solution)/shard_map/ppermute | solution.py:30
  86.3 0.4 copy.28
  86.7 0.9 multiply_reduce_fusion
  87.6 8.0 %all-reduce.2 = (f32[]{:T(128)}, f32[]{:T(128)}) all-reduce(f32[]{:T(128)} %multiply_reduce_fusion, f32[]{:T(128)} %get-tuple-element.406), channel_id=1, replica_groups=mesh['grp'=4,'elem_0'=4,'elem_1'=4,'elem_2'=2] {'grp'}, use_global_device_ids=true, to_apply=%region_6.7 | all-reduce | flops 2 | bytes 16 | tf_op jit(solution)/shard_map/psum | solution.py:34
  95.6 7.9 %all-reduce.1 = (f32[]{:T(128)}, f32[]{:T(128)}) all-reduce(f32[]{:T(128)} %get-tuple-element.455, f32[]{:T(128)} %get-tuple-element.456), channel_id=1, replica_groups=mesh['grp'=4,'elem_0'=4,'elem_1'=4,'elem_2'=2] {'elem_0'}, use_global_device_ids=true, to_apply=%region_7.8 | all-reduce | flops 2 | bytes 16 | tf_op jit(solution)/shard_map/psum | solution.py:34
  103.5 10.8 %all-reduce = (f32[]{:T(128)}, f32[]{:T(128)}) all-reduce(f32[]{:T(128)} %get-tuple-element.453, f32[]{:T(128)} %get-tuple-element.454), channel_id=1, replica_groups=mesh['grp'=4,'elem_0'=4,'elem_1'=4,'elem_2'=2] {'elem_1'}, use_global_device_ids=true, to_apply=%region_8.9 | all-reduce | flops 2 | bytes 16 | tf_op jit(solution)/shard_map/psum | solution.py:34
  114.3 8.8 %all-reduce.3 = (f32[]{:T(128)}, f32[]{:T(128)}) all-reduce(f32[]{:T(128)} %get-tuple-element.451, f32[]{:T(128)} %get-tuple-element.452), channel_id=1, replica_groups=mesh['grp'=4,'elem_0'=4,'elem_1'=4,'elem_2'=2] {'elem_2'}, use_global_device_ids=true, to_apply=%region_9.10 | all-reduce | flops 2 | bytes 16 | tf_op jit(solution)/shard_map/psum | solution.py:34
  123.8 1.1 broadcast_multiply_fusion
  124.9 2.2 %copy.29 = f32[3,2048]{1,0:T(4,128)} copy(f32[3,2048]{0,1:T(8,128)} %broadcast_multiply_fusion) | data formatting | bytes 49152
  (36 shorter events, 3.1 us)
Async XLA Ops:
  0.6 28.1 %copy-start = (f32[343,343]{1,0:T(8,128)S(1)}, f32[343,343]{1,0:T(8,128)}, u32[]{:S(2)}) copy-start(f32[343,343]{1,0:T(8,128)} %constant.165) | copy-start | bytes 1411792
  0.6 33.2 %copy-start.5 = (f32[8,343]{1,0:T(8,128)S(1)}, f32[8,343]{1,0:T(8,128)}, u32[]{:S(2)}) copy-start(f32[8,343]{1,0:T(8,128)} %constant.173) | copy-start | bytes 32932
  0.7 33.5 %copy-start.4 = (f32[8,343]{1,0:T(8,128)S(1)}, f32[8,343]{1,0:T(8,128)}, u32[]{:S(2)}) copy-start(f32[8,343]{1,0:T(8,128)} %constant.169) | copy-start | bytes 32932
  0.7 34.5 %copy-start.3 = (f32[8,343]{1,0:T(8,128)S(1)}, f32[8,343]{1,0:T(8,128)}, u32[]{:S(2)}) copy-start(f32[8,343]{1,0:T(8,128)} %constant.171) | copy-start | bytes 32932
  0.7 29.7 %copy-start.1 = (f32[3,343,128]{2,1,0:T(8,128)S(1)}, f32[3,343,128]{2,1,0:T(8,128)}, u32[]{:S(2)}) copy-start(f32[3,343,128]{2,1,0:T(8,128)} %param.11) | copy-start | bytes 1580548
  5.5 30.7 %copy-start.7 = (f32[343,1]{0,1:T(1,128)S(1)}, f32[343,1]{0,1:T(1,128)}, u32[]{:S(2)}) copy-start(f32[343,1]{0,1:T(1,128)} %constant.174) | copy-start | bytes 4120
  9.1 27.5 %copy-start.6 = (s32[8,128]{1,0:T(8,128)S(1)}, s32[8,128]{1,0:T(8,128)}, u32[]{:S(2)}) copy-start(s32[8,128]{1,0:T(8,128)} %param.14) | copy-start | bytes 12292
  32.0 9.5 %copy-start.2 = (f32[3,128]{1,0:T(4,128)S(1)}, f32[3,128]{1,0:T(4,128)}, u32[]{:S(2)}) copy-start(f32[3,128]{1,0:T(4,128)} %param.12) | copy-start | bytes 4612
  79.5 5.0 %collective-permute-start = (f32[3,2048]{1,0:T(4,128)S(1)}, f32[3,2048]{1,0:T(4,128)S(1)}, u32[]{:S(2)}, u32[]{:S(2)}) collective-permute-start(f32[3,2048]{1,0:T(4,128)S(1)} %copy.25), channel_id=1, source_target_pairs={{0,31},{1,0},{2,1},{3,2},{4,3},{5,4},{6,5},{7,6},{8,7},{9,8},{10,9... | collective-permute-start | bytes 73736 | tf_op jit(solution)/shard_map/ppermute | solution.py:30
  82.4 3.9 %collective-permute-start.1 = (f32[3,2048]{1,0:T(4,128)S(1)}, f32[3,2048]{1,0:T(4,128)S(1)}, u32[]{:S(2)}, u32[]{:S(2)}) collective-permute-start(f32[3,2048]{1,0:T(4,128)S(1)} %copy.27), channel_id=1, source_target_pairs={{0,1},{1,2},{2,3},{3,4},{4,5},{5,6},{6,7},{7,8},{8,9},{9,10},{10,1... | collective-permute-start | bytes 73736 | tf_op jit(solution)/shard_map/ppermute | solution.py:30
where the time goes:
time: 130 us; the launch traced here: 129 us
  blocking collectives  46.9 us (36%)
  matrix products  32.6 us (25%)
  other arithmetic  21.2 us (16%)
  local copies, waits for them, and re-layouts  17.7 us (14%)
  between operations  4.18 us (3%)
  starting transfers between devices  3.45 us (3%)
  waiting for transfers between devices  1.95 us (2%)
    psum x4, blocking collectives, by_axis(): return functools.reduce(lax.psum, axes, array)  35.5 us
    dot_general x18, matrix products, gradient(): jnp.dot(directional[j], field[i], precision=highest) * factor[j][None, :]  30 us
    scatter-add x1, other arithmetic, step(): assembled = assembled.at[:, target.reshape(-1)].add(terms.reshape(3, -1))  14.6 us
    all_to_all x1, blocking collectives, sent_and_summed(): lax.all_to_all(parts, axis, split_axis=0, concat_axis=0, tiled=True)  11.4 us
    another operation x1, local copies, waits for them, and re-layouts, in_blocks(): array.reshape(*lengths[:dim], devices, lengths[dim] // devices, *lengths[...  7.62 us
    broadcast_in_dim x1, local copies, waits for them, and re-layouts, body(): init = (jnp.zeros((3, extent), jnp.float32), jnp.zeros((), jnp.float32))  4.85 us
    ppermute x2, starting transfers between devices, passed_along(): lax.ppermute(array, axis, [(i, (i + by) % devices) for i in range(devices)])  3.45 us
    unnamed x20, local copies, waits for them, and re-layouts  3.3 us
  transfers between devices with their start and end apart: 2, of which 2 were waited for; matrix products, arithmetic and copies ran while one was open for 1% of the time, Pallas kernels for 0%

commit v1 on v0

v1 whole, which is shorter than its diff:
```python
import functools

import jax
import jax.numpy as jnp
import numpy as np
from jax import lax
from jax.experimental import pallas as pl
from jax.experimental.pallas import tpu as pltpu
from jax.sharding import Mesh
from jax.sharding import PartitionSpec as P

P_SIZE = 7
NODES = P_SIZE**3
ND_DEV = 2048
LANES = 128
ELEM = ("elem_0", "elem_1", "elem_2")
GRP_ELEM = ("grp", "elem_0", "elem_1", "elem_2")
SENT = 40
WIDE = 256


def lobatto(degree):
    points = np.cos(np.pi * np.arange(degree + 1) / degree)
    for sweep in range(60):
        lower = np.ones(degree + 1)
        upper = points.copy()
        for order in range(2, degree + 1):
            lower, upper = (upper, ((2 * order - 1) * points * upper - (order - 1) * lower) / order)
        points = points - (points * upper - lower) / ((degree + 1) * upper)
    lower = np.ones(degree + 1)
    upper = points.copy()
    for order in range(2, degree + 1):
        lower, upper = (upper, ((2 * order - 1) * points * upper - (order - 1) * lower) / order)
    return (points[::-1].copy(), upper[::-1].copy())


def one_dimensional():
    degree = P_SIZE - 1
    points, values = lobatto(degree)
    weights = 2.0 / (degree * (degree + 1) * values**2)
    derivative = np.zeros((P_SIZE, P_SIZE))
    for i in range(P_SIZE):
        for j in range(P_SIZE):
            if i != j:
                derivative[i, j] = values[i] / (values[j] * (points[i] - points[j]))
    derivative[0, 0] = -degree * (degree + 1) / 4.0
    derivative[degree, degree] = degree * (degree + 1) / 4.0
    points[degree // 2] = 0.0
    derivative[degree // 2, degree // 2] = 0.0
    return (points, weights, derivative)


POINTS, WEIGHTS, DERIVATIVE = one_dimensional()
COLUMN, ACROSS, ALONG, SIGNS = 0, 56, 72, 88
TABLE_ROWS = 144


def table():
    rows = np.zeros((TABLE_ROWS, LANES), np.float32)
    for c in range(P_SIZE):
        rows[COLUMN + 8 * c : COLUMN + 8 * c + P_SIZE] = DERIVATIVE[:, c][:, None]
    rows[ACROSS : ACROSS + P_SIZE] = WEIGHTS[:, None]
    rows[ACROSS + 8 : ACROSS + 8 + P_SIZE] = (WEIGHTS * POINTS)[:, None]
    rows[ALONG : ALONG + P_SIZE] = WEIGHTS[:, None]
    rows[ALONG + 8 : ALONG + 8 + P_SIZE] = (WEIGHTS * POINTS)[:, None]
    for number, axes in enumerate(((0,), (1,), (2,), (0, 1), (0, 2), (1, 2), (0, 1, 2))):
        for vertex in range(8):
            sign = np.prod([2.0 * (vertex >> 2 - m & 1) - 1.0 for m in axes])
            rows[SIGNS + 8 * number + vertex] = sign / 8.0
    return rows


def along_vectors(f):
    half = P_SIZE // 2
    last = P_SIZE - 1
    even = [f[j] + f[last - j] for j in range(half)]
    odd = [f[j] - f[last - j] for j in range(half)]
    out = [None] * P_SIZE
    for i in range(half + 1):
        coef = DERIVATIVE[i]
        b = None
        for j in range(half):
            piece = float((coef[j] - coef[last - j]) / 2) * odd[j]
            b = piece if b is None else b + piece
        if i == half:
            out[i] = b
            continue
        a = float(coef[half]) * f[half]
        for j in range(half):
            a = a + float((coef[j] + coef[last - j]) / 2) * even[j]
        out[i] = b + a
        out[last - i] = b - a
    return out


def terms_kernel(count_ref, u_ref, w_ref, h_ref, map_ref, tab_ref, out_ref, ga_ref, gb_ref, mom_ref):
    n = P_SIZE
    fields = [(ref, i) for ref in (u_ref, w_ref) for i in range(3)]
    rows = pl.ds(0, n)

    def first(b, carry):
        for f, (ref, i) in enumerate(fields):
            slabs = [ref[i, pl.ds(a * n * n + b * n, n), :] for a in range(n)]
            for a, value in enumerate(along_vectors(slabs)):
                ga_ref[f, a, b, rows, :] = value
        return carry

    lax.fori_loop(0, n, first, 0)
    mom_ref[...] = jnp.zeros_like(mom_ref)

    h = h_ref[...]
    factor = [2.0 / h[j : j + 1] for j in range(3)]
    square = [f * f for f in factor]

    def second(a, carry):
        base = a * n * n
        for f, (ref, i) in enumerate(fields):
            slabs = [ref[i, pl.ds(base + b * n, n), :] for b in range(n)]
            for b, value in enumerate(along_vectors(slabs)):
                gb_ref[f, b, rows, :] = value
        sums = [[None, None] for _ in range(6)]
        spent = None
        for b in range(n):
            grads = []
            for f, (ref, i) in enumerate(fields):
                gc = None
                for c in range(n):
                    row = ref[i, pl.ds(base + b * n + c, 1), :]
                    piece = tab_ref[pl.ds(COLUMN + 8 * c, n), :] * row
                    gc = piece if gc is None else gc + piece
                grads.append([ga_ref[f, a, b, rows, :], gb_ref[f, b, rows, :], gc])
            gu, gw = grads[:3], grads[3:]

            def cross(c, j):
                return gu[0][c] * gw[0][j] + gu[1][c] * gw[1][j] + gu[2][c] * gw[2][j]

            pairs = [cross(0, 0), cross(1, 1), cross(2, 2)]
            pairs += [cross(c, j) + cross(j, c) for c, j in ((0, 1), (0, 2), (1, 2))]
            own = [gu[0][j] * gu[0][j] + gu[1][j] * gu[1][j] + gu[2][j] * gu[2][j] for j in range(3)]
            squared = own[0] * square[0] + own[1] * square[1] + own[2] * square[2]
            weight = float(WEIGHTS[b])
            slope = float(WEIGHTS[b] * POINTS[b])
            for s, value in enumerate(pairs):
                piece = weight * value
                sums[s][0] = piece if sums[s][0] is None else sums[s][0] + piece
                if b != n // 2:
                    piece = slope * value
                    sums[s][1] = piece if sums[s][1] is None else sums[s][1] + piece
            piece = weight * squared
            spent = piece if spent is None else spent + piece
        wa = tab_ref[pl.ds(ALONG + a, 1), :]
        wxa = tab_ref[pl.ds(ALONG + 8 + a, 1), :]
        for s in range(6):
            for r, scale in enumerate((wa, wxa)):
                for t in range(2):
                    at = s * 4 + r * 2 + t
                    mom_ref[at, rows, :] = mom_ref[at, rows, :] + scale * sums[s][t]
        mom_ref[24, rows, :] = mom_ref[24, rows, :] + wa * spent
        return carry

    lax.fori_loop(0, n, second, 0)

    jacobian = h[0:1] * h[1:2] * h[2:3] * 0.125
    lanes = lax.broadcasted_iota(jnp.int32, (1, LANES), 1)
    live = jacobian * (lanes < count_ref[0]).astype(jnp.float32)
    flat = tab_ref[pl.ds(ACROSS, n), :]
    slant = tab_ref[pl.ds(ACROSS + 8, n), :]
    signs = [tab_ref[pl.ds(SIGNS + 8 * i, 8), :] for i in range(7)]

    def moment(value, c):
        return jnp.sum(value * (slant if c else flat), axis=0, keepdims=True)

    def along(axis, part):
        others = [m for m in range(3) if m != axis]
        total = None
        for low in range(2):
            for high in range(2):
                powers = [0, 0, 0]
                powers[others[0]] = low
                powers[others[1]] = high
                axes = tuple(sorted([axis] + [m for m in others if powers[m]]))
                number = {(0,): 0, (1,): 1, (2,): 2, (0, 1): 3, (0, 2): 4, (1, 2): 5, (0, 1, 2): 6}[axes]
                piece = signs[number] * moment(part[powers[0] * 2 + powers[1]], powers[2])
                total = piece if total is None else total + piece
        return total

    mom = [[mom_ref[s * 4 + i, rows, :] for i in range(4)] for s in range(6)]
    inner = [
        square[0] * mom[0][i] + square[1] * mom[1][i] + square[2] * mom[2][i] for i in range(4)
    ]
    between = {(0, 1): 3, (0, 2): 4, (1, 2): 5}
    for c in range(3):
        part = [inner[i] - (2.0 * square[c]) * mom[c][i] for i in range(4)]
        total = along(c, part)
        for j in range(3):
            if j != c:
                shared = mom[between[(min(c, j), max(c, j))]]
                total = total - square[j] * along(j, shared)
        out_ref[pl.ds(8 * c, 8), :] = total * (factor[c] * live)
    out_ref[pl.ds(24, 8), :] = map_ref[...].astype(jnp.float32)
    spent = live * moment(mom_ref[24, rows, :], 0)
    out_ref[pl.ds(32, 8), :] = jnp.broadcast_to(spent, (8, LANES))


def element_terms(count, velocity, adjoint, spacing, design_map):
    vmem = pl.BlockSpec(memory_space=pltpu.VMEM)
    return pl.pallas_call(
        terms_kernel,
        out_shape=jax.ShapeDtypeStruct((SENT, LANES), jnp.float32),
        in_specs=[pl.BlockSpec(memory_space=pltpu.SMEM)] + [vmem] * 5,
        out_specs=vmem,
        scratch_shapes=[
            pltpu.VMEM((6, P_SIZE, P_SIZE, 8, LANES), jnp.float32),
            pltpu.VMEM((6, P_SIZE, 8, LANES), jnp.float32),
            pltpu.VMEM((25, 8, LANES), jnp.float32),
        ],
        compiler_params=pltpu.CompilerParams(vmem_limit_bytes=32 * 1024 * 1024),
    )(count, velocity, adjoint, spacing, design_map, jnp.asarray(table()))


def assemble_kernel(groups, columns, place_ref, own_ref, *refs):
    others = refs[: groups - 1]
    grad_ref, part_ref, left_ref, right_ref, sum_ref = refs[groups - 1 :]
    group = place_ref[0]
    column = place_ref[1]
    per_owner = ND_DEV // WIDE
    high = groups * per_owner
    iota_wide = lax.broadcasted_iota(jnp.int32, (WIDE, LANES), 0)
    iota_high = lax.broadcasted_iota(jnp.int32, (high, LANES), 0)
    sum_ref[...] = jnp.zeros_like(sum_ref)
    for source in (own_ref, *others):

        def add(s, carry):
            for k in range(8):
                node = source[s, pl.ds(24 + k, 1), :].astype(jnp.int32)
                owner = node // ND_DEV
                mine = owner % columns == column
                low = node % WIDE
                at = (owner // columns) * per_owner + (node % ND_DEV) // WIDE
                at = jnp.where(mine, at, -1)
                lanes = pl.ds(k * LANES, LANES)
                right_ref[:, lanes] = jnp.where(iota_wide == low, 1.0, 0.0).astype(jnp.bfloat16)
                hit = iota_high == at
                for c in range(3):
                    value = source[s, pl.ds(8 * c + k, 1), :]
                    coarse = value.astype(jnp.bfloat16).astype(jnp.float32)
                    for piece, part in enumerate((coarse, value - coarse)):
                        row = (piece * 3 + c) * high
                        left_ref[pl.ds(row, high), lanes] = jnp.where(hit, part, 0.0).astype(
                            jnp.bfloat16
                        )
            sum_ref[...] += lax.dot_general(
                left_ref[...],
                right_ref[...],
                (((1,), (1,)), ((), ())),
                preferred_element_type=jnp.float32,
            )
            return carry

        lax.fori_loop(0, 3, add, 0)
    total = sum_ref[pl.ds(0, 3 * high), :] + sum_ref[pl.ds(3 * high, 3 * high), :]
    squares = jnp.sum(total * total)
    sum_ref[pl.ds(0, 3 * high), :] = total
    for c in range(3):
        block = sum_ref[pl.ds(c * high + group * per_owner, per_owner), :]
        for i in range(per_owner):
            grad_ref[c : c + 1, i * WIDE : (i + 1) * WIDE] = block[i : i + 1, :]
    spent = own_ref[0, pl.ds(32, 1), :]
    for other in others:
        spent = spent + other[0, pl.ds(32, 1), :]
    spent = jnp.sum(spent)
    lane = lax.broadcasted_iota(jnp.int32, (1, LANES), 1)
    stats = jnp.where(lane == 0, squares, jnp.where(lane == 1, spent, 0.0))
    part_ref[...] = jnp.broadcast_to(stats[None], part_ref.shape)


def assembled(place, arrays, columns):
    groups = len(arrays)
    high = groups * (ND_DEV // WIDE)
    vmem = pl.BlockSpec(memory_space=pltpu.VMEM)
    return pl.pallas_call(
        functools.partial(assemble_kernel, groups, columns),
        out_shape=(
            jax.ShapeDtypeStruct((3, ND_DEV), jnp.float32),
            jax.ShapeDtypeStruct((columns, 1, LANES), jnp.float32),
        ),
        in_specs=[pl.BlockSpec(memory_space=pltpu.SMEM)] + [vmem] * groups,
        out_specs=(vmem, vmem),
        scratch_shapes=[
            pltpu.VMEM((6 * high, 8 * LANES), jnp.bfloat16),
            pltpu.VMEM((WIDE, 8 * LANES), jnp.bfloat16),
            pltpu.VMEM((6 * high, WIDE), jnp.float32),
        ],
        compiler_params=pltpu.CompilerParams(vmem_limit_bytes=32 * 1024 * 1024),
    )(place, *arrays)


def scale_kernel(over_nodes, over_elements, grad_ref, part_ref, out_ref, objective_ref):
    total = jnp.sum(part_ref[:, 0, :], axis=0, keepdims=True)
    lane = lax.broadcasted_iota(jnp.int32, (1, LANES), 1)
    squares = jnp.sum(jnp.where(lane == 0, total, 0.0), axis=1, keepdims=True)
    spent = jnp.sum(jnp.where(lane == 1, total, 0.0), axis=1, keepdims=True)
    out_ref[...] = grad_ref[...] * lax.rsqrt(squares * over_nodes + 1e-06)
    objective_ref[...] = spent * over_elements


def scaled(grad, parts, over_nodes, over_elements):
    vmem = pl.BlockSpec(memory_space=pltpu.VMEM)
    return pl.pallas_call(
        functools.partial(scale_kernel, over_nodes, over_elements),
        out_shape=(
            jax.ShapeDtypeStruct((3, ND_DEV), jnp.float32),
            jax.ShapeDtypeStruct((1, 1), jnp.float32),
        ),
        in_specs=[vmem, vmem],
        out_specs=(vmem, vmem),
    )(grad, parts)


def shifted(array, axis, by):
    devices = lax.axis_size(axis)
    return lax.ppermute(array, axis, [(i, (i + by) % devices) for i in range(devices)])


def body(velocity, adjoint, spacing, elem_count, design_map):
    slots = velocity.shape[-1]
    groups = lax.axis_size("grp")
    columns = lax.axis_size(ELEM)
    sent = element_terms(elem_count, velocity, adjoint, spacing, design_map)
    within = lax.ppermute(sent, "elem_2", [(0, 1), (1, 0)])
    partner = [(e + 1) % columns if e % 2 else (e - 1) % columns for e in range(columns)]
    across = lax.ppermute(sent, ELEM, list(enumerate(partner)))
    three = jnp.stack([sent, within, across])
    arrays = [three] + [shifted(three, "grp", by) for by in range(1, groups)]
    place = jnp.stack([lax.axis_index("grp"), lax.axis_index(ELEM)]).astype(jnp.int32)
    grad, parts = assembled(place, arrays, columns)
    parts = lax.all_to_all(parts, ELEM, split_axis=0, concat_axis=0, tiled=True)
    devices = groups * columns
    direction, objective = scaled(
        grad,
        parts,
        1.0 / (3.0 * ND_DEV * devices),
        1.0 / (NODES * slots * devices),
    )
    return (direction, objective.reshape(()))


def solution(mesh):
    finer = Mesh(
        mesh.devices.reshape(mesh.shape["grp"], 4, 4, 2), ("grp", "elem_0", "elem_1", "elem_2")
    )
    in_specs = (
        P(None, None, GRP_ELEM),
        P(None, None, GRP_ELEM),
        P(None, GRP_ELEM),
        P(GRP_ELEM),
        P(None, GRP_ELEM),
    )
    out_specs = (P(None, GRP_ELEM), P())
    return jax.shard_map(body, mesh=finer, in_specs=in_specs, out_specs=out_specs, check_vma=False)
```

time: 130 us -> 47.3 us (0.36)
  blocking collectives: 46.9 us -> 14 us
  matrix products: 32.6 us -> 0 us
  other arithmetic: 21.2 us -> 0.08 us
  local copies, waits for them, and re-layouts: 17.7 us -> 4.94 us
  Pallas kernels: 0 us -> 10.8 us
  starting transfers between devices: 3.45 us -> 10.7 us
  waiting for transfers between devices: 1.95 us -> 5.01 us
  between operations: 4.18 us -> 1.31 us
    psum x4 -> x0, blocking collectives: 35.5 us -> none  [by_axis(): return functools.reduce(lax.psum, axes, array)]
    dot_general x28 -> x0, matrix products: 32.6 us -> none  [the longest x18 30 us: gradient(): jnp.dot(directional[j], field[i], precision=highest) * factor[j][None, :]]
    scatter-add x1 -> x0, other arithmetic: 14.6 us -> none  [step(): assembled = assembled.at[:, target.reshape(-1)].add(terms.reshape(3, -1))]
    pallas_call x0 -> x3, Pallas kernels: none -> 10.8 us  [the longest x1 7.36 us: assembled(): pl.pallas_call(functools.partial(assemble_kernel, groups, columns), out_s...]
    another operation x1 -> x0, local copies, waits for them, and re-layouts: 7.62 us -> none  [in_blocks(): array.reshape(*lengths[:dim], devices, lengths[dim] // devices, *lengths[...]
    ppermute x2 -> x5, starting transfers between devices: 3.45 us -> 10.7 us  [the longest x3 4.46 us: shifted(): lax.ppermute(array, axis, [(i, (i + by) % devices) for i in range(devices)])]
    broadcast_in_dim x1 -> x0, local copies, waits for them, and re-layouts: 4.85 us -> none  [body(): init = (jnp.zeros((3, extent), jnp.float32), jnp.zeros((), jnp.float32))]
    ppermute x2 -> x5, waiting for transfers between devices: 1.95 us -> 5.01 us  [the longest x3 4.17 us: shifted(): lax.ppermute(array, axis, [(i, (i + by) % devices) for i in range(devices)])]
  transfers between devices with their start and end apart: 2 -> 5, of which waited for: 2 -> 4; matrix products, arithmetic and copies ran while one was open for 1% -> 0% of each run, Pallas kernels for 0% -> 0%
where the time goes in v1:
time: 47.3 us; the launch traced here: 46.8 us
  blocking collectives  14 us (30%)
  Pallas kernels  10.8 us (23%)
  starting transfers between devices  10.7 us (23%)
  waiting for transfers between devices  5.01 us (11%)
  local copies, waits for them, and re-layouts  4.94 us (10%)
  between operations  1.31 us (3%)
    all_to_all x1, blocking collectives, body(): parts = lax.all_to_all(parts, ELEM, split_axis=0, concat_axis=0, tiled=True)  14 us
    pallas_call x1, Pallas kernels, assembled(): pl.pallas_call(functools.partial(assemble_kernel, groups, columns), out_s...  7.36 us
    unnamed x12, local copies, waits for them, and re-layouts  4.94 us
    ppermute x3, starting transfers between devices, shifted(): lax.ppermute(array, axis, [(i, (i + by) % devices) for i in range(devices)])  4.46 us
    ppermute x3, waiting for transfers between devices, shifted(): lax.ppermute(array, axis, [(i, (i + by) % devices) for i in range(devices)])  4.17 us
    ppermute x1, starting transfers between devices, body(): within = lax.ppermute(sent, 'elem_2', [(0, 1), (1, 0)])  3.47 us
    ppermute x1, starting transfers between devices, body(): across = lax.ppermute(sent, ELEM, list(enumerate(partner)))  2.77 us
    pallas_call x1, Pallas kernels, element_terms(): pl.pallas_call(terms_kernel, out_shape=jax.ShapeDtypeStruct((SENT, LANES)...  1.92 us
  transfers between devices with their start and end apart: 5, of which 4 were waited for; matrix products, arithmetic and copies ran while one was open for 0% of the time, Pallas kernels for 0%

profile of v1, /device:TPU:1, one launch (start us, length us, event | category | flops | bytes accessed | tf_op | source)
XLA Modules:
  0.0 46.8 jit_solution(2953148310070359173)
XLA Ops:
  1.3 0.0 copy-start
  1.3 1.0 %copy-done = f32[3,343,128]{2,1,0:T(8,128)S(1)} copy-done((f32[3,343,128]{2,1,0:T(8,128)S(1)}, f32[3,343,128]{2,1,0:T(8,128)}, u32[]{:S(2)}) %copy-start) | copy-done | bytes 526872
  2.3 0.0 copy-start.1
  2.3 1.0 %copy-done.1 = f32[3,343,128]{2,1,0:T(8,128)S(1)} copy-done((f32[3,343,128]{2,1,0:T(8,128)S(1)}, f32[3,343,128]{2,1,0:T(8,128)}, u32[]{:S(2)}) %copy-start.1) | copy-done | bytes 526872
  3.4 0.0 copy-start.2
  3.4 0.9 %copy-done.2 = f32[144,128]{1,0:T(8,128)S(1)} copy-done((f32[144,128]{1,0:T(8,128)S(1)}, f32[144,128]{1,0:T(8,128)}, u32[]{:S(2)}) %copy-start.2) | copy-done | bytes 73752
  4.2 0.0 copy-start.4
  4.3 0.7 %copy-done.4 = s32[8,128]{1,0:T(8,128)S(1)} copy-done((s32[8,128]{1,0:T(8,128)S(1)}, s32[8,128]{1,0:T(8,128)}, u32[]{:S(2)}) %copy-start.4) | copy-done | bytes 4120
  4.9 0.0 copy-start.5
  4.9 0.7 %copy-done.5 = f32[3,128]{1,0:T(4,128)S(1)} copy-done((f32[3,128]{1,0:T(4,128)S(1)}, f32[3,128]{1,0:T(4,128)}, u32[]{:S(2)}) %copy-start.5) | copy-done | bytes 1560
  5.6 1.9 %shard_map.77 = f32[40,128]{1,0:T(8,128)S(1)} custom-call(s32[1]{0:T(128)S(6)} %copy.8.count_ref, f32[3,343,128]{2,1,0:T(8,128)S(1)} %copy-done, f32[3,343,128]{2,1,0:T(8,128)S(1)} %copy-done.1, f32[3,128]{1,0:T(4,128)S(1)} %copy-done.5, s32[8,128]{1,0:T(8,128)S(1)} %copy-done.4, f32[144,128]{1,0:T(8,128)S(1)} %copy-done.2), custom_call_target="tpu_custom_call" | custom-call | tf_op jit(solution)/shard_map/pallas_call | solution.py:207
  7.5 2.8 %collective-permute-start.1 = (f32[40,128]{1,0:T(8,128)S(1)}, f32[40,128]{1,0:T(8,128)S(1)}, u32[]{:S(2)}, u32[]{:S(2)}) collective-permute-start(f32[40,128]{1,0:T(8,128)S(1)} %shard_map.77), channel_id=1, source_target_pairs={{0,31},{1,2},{2,1},{3,4},{4,3},{5,6},{6,5},{7,8},{8,7},{9,10},{10,... | collective-permute-start | bytes 61448 | tf_op jit(solution)/shard_map/ppermute | solution.py:332
  10.3 3.5 %collective-permute-start = (f32[40,128]{1,0:T(8,128)S(1)}, f32[40,128]{1,0:T(8,128)S(1)}, u32[]{:S(2)}, u32[]{:S(2)}) collective-permute-start(f32[40,128]{1,0:T(8,128)S(1)} %shard_map.77), channel_id=1, source_target_pairs={{0,1},{1,0},{2,3},{3,2},{4,5},{5,4},{6,7},{7,6},{8,9},{9,8},{10,11... | collective-permute-start | bytes 61448 | tf_op jit(solution)/shard_map/ppermute | solution.py:330
  13.8 0.0 collective-permute-done.1
  13.8 0.8 %collective-permute-done = f32[40,128]{1,0:T(8,128)S(1)} collective-permute-done((f32[40,128]{1,0:T(8,128)S(1)}, f32[40,128]{1,0:T(8,128)S(1)}, u32[]{:S(2)}, u32[]{:S(2)}) %collective-permute-start) | collective-permute-done | bytes 20512 | tf_op jit(solution)/shard_map/ppermute | solution.py:330
  14.6 3.8 %collective-permute-start.4 = (f32[3,40,128]{2,1,0:T(8,128)S(1)}, f32[3,40,128]{2,1,0:T(8,128)S(1)}, u32[]{:S(2)}, u32[]{:S(2)}) collective-permute-start(f32[3,40,128]{2,1,0:T(8,128)S(1)} %pad_maximum_fusion.own_ref), channel_id=1, source_target_pairs={{0,96},{32,0},{64,32},{96,64},{1,97},{33,1},{65,33},{97,65},{2,98}... | collective-permute-start | bytes 184328 | tf_op jit(solution)/shard_map/ppermute | solution.py:322
  18.4 0.0 collective-permute-start.3
  18.4 0.7 %collective-permute-start.2 = (f32[3,40,128]{2,1,0:T(8,128)S(1)}, f32[3,40,128]{2,1,0:T(8,128)S(1)}, u32[]{:S(2)}, u32[]{:S(2)}) collective-permute-start(f32[3,40,128]{2,1,0:T(8,128)S(1)} %pad_maximum_fusion.own_ref), channel_id=1, source_target_pairs={{0,32},{32,64},{64,96},{96,0},{1,33},{33,65},{65,97},{97,1},{2,34}... | collective-permute-start | bytes 184328 | tf_op jit(solution)/shard_map/ppermute | solution.py:322
  19.1 0.1 pad_add_fusion.place_ref
  19.2 0.5 %collective-permute-done.4.refs_2_ = f32[3,40,128]{2,1,0:T(8,128)S(1)} collective-permute-done((f32[3,40,128]{2,1,0:T(8,128)S(1)}, f32[3,40,128]{2,1,0:T(8,128)S(1)}, u32[]{:S(2)}, u32[]{:S(2)}) %collective-permute-start.4) | collective-permute-done | bytes 61472 | tf_op jit(solution)/shard_map/ppermute | solution.py:322
  19.7 3.4 %collective-permute-done.3.refs_1_ = f32[3,40,128]{2,1,0:T(8,128)S(1)} collective-permute-done((f32[3,40,128]{2,1,0:T(8,128)S(1)}, f32[3,40,128]{2,1,0:T(8,128)S(1)}, u32[]{:S(2)}, u32[]{:S(2)}) %collective-permute-start.3) | collective-permute-done | bytes 61472 | tf_op jit(solution)/shard_map/ppermute | solution.py:322
  23.1 0.3 collective-permute-done.2.refs_0_
  23.3 7.4 %shard_map.78 = (f32[3,2048]{1,0:T(4,128)S(1)}, f32[32,1,128]{2,1,0:T(1,128)S(1)}) custom-call(s32[2]{0:T(128)S(1)} %pad_add_fusion.place_ref, f32[3,40,128]{2,1,0:T(8,128)S(1)} %pad_maximum_fusion.own_ref, f32[3,40,128]{2,1,0:T(8,128)S(1)} %collective-permute-done.2.refs_0_, f32[3,40,128]{2,1,0:T(8,128)S(1)} %collective-permute-done.3.refs_1_, ...), custom_call_target="tpu_custom_call" | custom-call | tf_op jit(solution)/shard_map/pallas_call | solution.py:281
  30.7 0.0 copy-start.3
  30.7 0.6 %copy-done.3 = f32[3,2048]{1,0:T(4,128)} copy-done((f32[3,2048]{1,0:T(4,128)}, f32[3,2048]{1,0:T(4,128)S(1)}, u32[]{:S(2)}) %copy-start.3) | copy-done | bytes 24600
  31.3 14.0 %all_to_all.5.part_ref = f32[32,1,128]{2,1,0:T(1,128)} all-to-all(f32[32,1,128]{2,1,0:T(1,128)S(1)} %get-tuple-element.7), channel_id=1, replica_groups=mesh['grp'=4,'elem_0'=4,'elem_1'=4,'elem_2'=2] {'elem_0','elem_1','elem_2'}, dimensions={0} | all-to-all | bytes 32768 | tf_op jit(solution)/shard_map/all_to_all | solution.py:337
  45.4 1.5 %shard_map.79 = (f32[3,2048]{1,0:T(4,128)}, f32[1,1]{1,0:T(1,128)}) custom-call(f32[3,2048]{1,0:T(4,128)} %copy-done.3, f32[32,1,128]{2,1,0:T(1,128)} %all_to_all.5.part_ref), custom_call_target="tpu_custom_call" | custom-call | tf_op jit(solution)/shard_map/pallas_call | solution.py:309
  (1 shorter events, 0.0 us)
Async XLA Ops:
  1.3 1.0 %copy-start = (f32[3,343,128]{2,1,0:T(8,128)S(1)}, f32[3,343,128]{2,1,0:T(8,128)}, u32[]{:S(2)}) copy-start(f32[3,343,128]{2,1,0:T(8,128)} %u_ref.1) | copy-start | bytes 1580548
  2.3 1.0 %copy-start.1 = (f32[3,343,128]{2,1,0:T(8,128)S(1)}, f32[3,343,128]{2,1,0:T(8,128)}, u32[]{:S(2)}) copy-start(f32[3,343,128]{2,1,0:T(8,128)} %w_ref.1) | copy-start | bytes 1580548
  3.4 0.9 %copy-start.2 = (f32[144,128]{1,0:T(8,128)S(1)}, f32[144,128]{1,0:T(8,128)}, u32[]{:S(2)}) copy-start(f32[144,128]{1,0:T(8,128)} %constant.21.clone.tab_ref) | copy-start | bytes 221188
  4.2 0.7 %copy-start.4 = (s32[8,128]{1,0:T(8,128)S(1)}, s32[8,128]{1,0:T(8,128)}, u32[]{:S(2)}) copy-start(s32[8,128]{1,0:T(8,128)} %map_ref.1) | copy-start | bytes 12292
  4.9 0.7 %copy-start.5 = (f32[3,128]{1,0:T(4,128)S(1)}, f32[3,128]{1,0:T(4,128)}, u32[]{:S(2)}) copy-start(f32[3,128]{1,0:T(4,128)} %h_ref.1) | copy-start | bytes 4612
  7.5 6.2 %collective-permute-start.1 = (f32[40,128]{1,0:T(8,128)S(1)}, f32[40,128]{1,0:T(8,128)S(1)}, u32[]{:S(2)}, u32[]{:S(2)}) collective-permute-start(f32[40,128]{1,0:T(8,128)S(1)} %shard_map.77), channel_id=1, source_target_pairs={{0,31},{1,2},{2,1},{3,4},{4,3},{5,6},{6,5},{7,8},{8,7},{9,10},{10,... | collective-permute-start | bytes 61448 | tf_op jit(solution)/shard_map/ppermute | solution.py:332
  10.3 4.3 %collective-permute-start = (f32[40,128]{1,0:T(8,128)S(1)}, f32[40,128]{1,0:T(8,128)S(1)}, u32[]{:S(2)}, u32[]{:S(2)}) collective-permute-start(f32[40,128]{1,0:T(8,128)S(1)} %shard_map.77), channel_id=1, source_target_pairs={{0,1},{1,0},{2,3},{3,2},{4,5},{5,4},{6,7},{7,6},{8,9},{9,8},{10,11... | collective-permute-start | bytes 61448 | tf_op jit(solution)/shard_map/ppermute | solution.py:330
  14.6 5.1 %collective-permute-start.4 = (f32[3,40,128]{2,1,0:T(8,128)S(1)}, f32[3,40,128]{2,1,0:T(8,128)S(1)}, u32[]{:S(2)}, u32[]{:S(2)}) collective-permute-start(f32[3,40,128]{2,1,0:T(8,128)S(1)} %pad_maximum_fusion.own_ref), channel_id=1, source_target_pairs={{0,96},{32,0},{64,32},{96,64},{1,97},{33,1},{65,33},{97,65},{2,98}... | collective-permute-start | bytes 184328 | tf_op jit(solution)/shard_map/ppermute | solution.py:322
  18.4 4.7 %collective-permute-start.3 = (f32[3,40,128]{2,1,0:T(8,128)S(1)}, f32[3,40,128]{2,1,0:T(8,128)S(1)}, u32[]{:S(2)}, u32[]{:S(2)}) collective-permute-start(f32[3,40,128]{2,1,0:T(8,128)S(1)} %pad_maximum_fusion.own_ref), channel_id=1, source_target_pairs={{0,64},{32,96},{64,0},{96,32},{1,65},{33,97},{65,1},{97,33},{2,66}... | collective-permute-start | bytes 184328 | tf_op jit(solution)/shard_map/ppermute | solution.py:322
  18.4 4.9 %collective-permute-start.2 = (f32[3,40,128]{2,1,0:T(8,128)S(1)}, f32[3,40,128]{2,1,0:T(8,128)S(1)}, u32[]{:S(2)}, u32[]{:S(2)}) collective-permute-start(f32[3,40,128]{2,1,0:T(8,128)S(1)} %pad_maximum_fusion.own_ref), channel_id=1, source_target_pairs={{0,32},{32,64},{64,96},{96,0},{1,33},{33,65},{65,97},{97,1},{2,34}... | collective-permute-start | bytes 184328 | tf_op jit(solution)/shard_map/ppermute | solution.py:322
  30.7 0.6 %copy-start.3 = (f32[3,2048]{1,0:T(4,128)}, f32[3,2048]{1,0:T(4,128)S(1)}, u32[]{:S(2)}) copy-start(f32[3,2048]{1,0:T(4,128)S(1)} %get-tuple-element.6.grad_ref) | copy-start | bytes 73732

commit v2 on v1

--- a/solution.py
+++ b/solution.py
@@ -93,20 +93,61 @@
     return out
 
 
-def terms_kernel(count_ref, u_ref, w_ref, h_ref, map_ref, tab_ref, out_ref, ga_ref, gb_ref, mom_ref):
+def terms_kernel(
+    count_ref,
+    u_hbm,
+    w_hbm,
+    h_hbm,
+    map_hbm,
+    tab_hbm,
+    out_ref,
+    u_ref,
+    w_ref,
+    h_ref,
+    map_ref,
+    tab_ref,
+    ga_ref,
+    gb_ref,
+    mom_ref,
+    sems,
+):
     n = P_SIZE
     fields = [(ref, i) for ref in (u_ref, w_ref) for i in range(3)]
     rows = pl.ds(0, n)
-
-    def first(b, carry):
-        for f, (ref, i) in enumerate(fields):
-            slabs = [ref[i, pl.ds(a * n * n + b * n, n), :] for a in range(n)]
-            for a, value in enumerate(along_vectors(slabs)):
-                ga_ref[f, a, b, rows, :] = value
-        return carry
-
-    lax.fori_loop(0, n, first, 0)
+    pairs = (
+        (u_hbm, u_ref),
+        (w_hbm, w_ref),
+        (tab_hbm, tab_ref),
+        (h_hbm, h_ref),
+        (map_hbm, map_ref),
+    )
+    copies = [
+        pltpu.make_async_copy(source, target, sems.at[i])
+        for i, (source, target) in enumerate(pairs)
+    ]
+    for copy in copies:
+        copy.start()
+
+    def first(f, ref, i, b):
+        slabs = [ref[i, pl.ds(a * n * n + b * n, n), :] for a in range(n)]
+        for a, value in enumerate(along_vectors(slabs)):
+            ga_ref[f, a, b, rows, :] = value
+
+    def half(start):
+        def step(b, carry):
+            for f in range(start, start + 3):
+                first(f, *fields[f], b)
+            return carry
+
+        lax.fori_loop(0, n, step, 0)
+
     mom_ref[...] = jnp.zeros_like(mom_ref)
+    copies[0].wait()
+    half(0)
+    copies[1].wait()
+    half(3)
+    for copy in copies[2:]:
+        copy.wait()
 
     h = h_ref[...]
     factor = [2.0 / h[j : j + 1] for j in range(3)]
@@ -204,95 +245,126 @@
 
 def element_terms(count, velocity, adjoint, spacing, design_map):
     vmem = pl.BlockSpec(memory_space=pltpu.VMEM)
+    arrays = (velocity, adjoint, spacing, design_map, jnp.asarray(table()))
+    arrays = [pltpu.with_memory_space_constraint(array, pltpu.HBM) for array in arrays]
     return pl.pallas_call(
         terms_kernel,
-        out_shape=jax.ShapeDtypeStruct((SENT, LANES), jnp.float32),
-        in_specs=[pl.BlockSpec(memory_space=pltpu.SMEM)] + [vmem] * 5,
+        out_shape=pltpu.VMEM((SENT, LANES), jnp.float32),
+        in_specs=[pl.BlockSpec(memory_space=pltpu.SMEM)]
+        + [pl.BlockSpec(memory_space=pltpu.HBM)] * 5,
         out_specs=vmem,
         scratch_shapes=[
+            pltpu.VMEM(velocity.shape, jnp.float32),
+            pltpu.VMEM(adjoint.shape, jnp.float32),
+            pltpu.VMEM(spacing.shape, jnp.float32),
+            pltpu.VMEM(design_map.shape, jnp.int32),
+            pltpu.VMEM((TABLE_ROWS, LANES), jnp.float32),
             pltpu.VMEM((6, P_SIZE, P_SIZE, 8, LANES), jnp.float32),
             pltpu.VMEM((6, P_SIZE, 8, LANES), jnp.float32),
             pltpu.VMEM((25, 8, LANES), jnp.float32),
+            pltpu.SemaphoreType.DMA((5,)),
         ],
-        compiler_params=pltpu.CompilerParams(vmem_limit_bytes=32 * 1024 * 1024),
-    )(count, velocity, adjoint, spacing, design_map, jnp.asarray(table()))
-
-
-def assemble_kernel(groups, columns, place_ref, own_ref, *refs):
-    others = refs[: groups - 1]
-    grad_ref, part_ref, left_ref, right_ref, sum_ref = refs[groups - 1 :]
-    group = place_ref[0]
-    column = place_ref[1]
+        compiler_params=pltpu.CompilerParams(vmem_limit_bytes=16 * 1024 * 1024),
+    )(count, *arrays)
+
+
+def spread_kernel(groups, columns, adds, column_ref, source, *refs):
+    base_ref = refs[0] if adds else None
+    sum_ref, left_ref, right_ref = refs[-3:]
+    column = column_ref[0]
     per_owner = ND_DEV // WIDE
     high = groups * per_owner
     iota_wide = lax.broadcasted_iota(jnp.int32, (WIDE, LANES), 0)
     iota_high = lax.broadcasted_iota(jnp.int32, (high, LANES), 0)
-    sum_ref[...] = jnp.zeros_like(sum_ref)
-    for source in (own_ref, *others):
-
-        def add(s, carry):
-            for k in range(8):
-                node = source[s, pl.ds(24 + k, 1), :].astype(jnp.int32)
-                owner = node // ND_DEV
-                mine = owner % columns == column
-                low = node % WIDE
-                at = (owner // columns) * per_owner + (node % ND_DEV) // WIDE
-                at = jnp.where(mine, at, -1)
-                lanes = pl.ds(k * LANES, LANES)
-                right_ref[:, lanes] = jnp.where(iota_wide == low, 1.0, 0.0).astype(jnp.bfloat16)
-                hit = iota_high == at
-                for c in range(3):
-                    value = source[s, pl.ds(8 * c + k, 1), :]
-                    coarse = value.astype(jnp.bfloat16).astype(jnp.float32)
-                    for piece, part in enumerate((coarse, value - coarse)):
-                        row = (piece * 3 + c) * high
-                        left_ref[pl.ds(row, high), lanes] = jnp.where(hit, part, 0.0).astype(
-                            jnp.bfloat16
-                        )
-            sum_ref[...] += lax.dot_general(
-                left_ref[...],
-                right_ref[...],
-                (((1,), (1,)), ((), ())),
-                preferred_element_type=jnp.float32,
-            )
-            return carry
-
-        lax.fori_loop(0, 3, add, 0)
-    total = sum_ref[pl.ds(0, 3 * high), :] + sum_ref[pl.ds(3 * high, 3 * high), :]
-    squares = jnp.sum(total * total)
-    sum_ref[pl.ds(0, 3 * high), :] = total
-    for c in range(3):
-        block = sum_ref[pl.ds(c * high + group * per_owner, per_owner), :]
-        for i in range(per_owner):
-            grad_ref[c : c + 1, i * WIDE : (i + 1) * WIDE] = block[i : i + 1, :]
-    spent = own_ref[0, pl.ds(32, 1), :]
-    for other in others:
-        spent = spent + other[0, pl.ds(32, 1), :]
-    spent = jnp.sum(spent)
+    for k in range(8):
+        node = source[pl.ds(24 + k, 1), :].astype(jnp.int32)
+        owner = node // ND_DEV
+        mine = owner % columns == column
+        low = node % WIDE
+        at = (owner // columns) * per_owner + (node % ND_DEV) // WIDE
+        at = jnp.where(mine, at, -1)
+        lanes = pl.ds(k * LANES, LANES)
+        right_ref[:, lanes] = jnp.where(iota_wide == low, 1.0, 0.0).astype(jnp.bfloat16)
+        hit = iota_high == at
+        for c in range(3):
+            value = source[pl.ds(8 * c + k, 1), :]
+            coarse = value.astype(jnp.bfloat16).astype(jnp.float32)
+            for piece, part in enumerate((coarse, value - coarse)):
+                row = (piece * 3 + c) * high
+                left_ref[pl.ds(row, high), lanes] = jnp.where(hit, part, 0.0).astype(jnp.bfloat16)
+    both = lax.dot_general(
+        left_ref[...],
+        right_ref[...],
+        (((1,), (1,)), ((), ())),
+        preferred_element_type=jnp.float32,
+    )
+    total = both[: 3 * high] + both[3 * high :]
+    rest = pl.ds(3 * high, 8)
+    if adds:
+        sum_ref[pl.ds(0, 3 * high), :] = base_ref[pl.ds(0, 3 * high), :] + total
+        sum_ref[rest, :] = base_ref[rest, :]
+    else:
+        sum_ref[pl.ds(0, 3 * high), :] = total
+        sum_ref[rest, 0:LANES] = source[pl.ds(32, 8), :]
+        sum_ref[rest, LANES:WIDE] = jnp.zeros((8, WIDE - LANES), jnp.float32)
+
+
+def spread(column, source, base, groups, columns):
+    high = groups * (ND_DEV // WIDE)
+    vmem = pl.BlockSpec(memory_space=pltpu.VMEM)
+    bases = () if base is None else (base,)
+    return pl.pallas_call(
+        functools.partial(spread_kernel, groups, columns, base is not None),
+        out_shape=jax.ShapeDtypeStruct((3 * high + 8, WIDE), jnp.float32),
+        in_specs=[pl.BlockSpec(memory_space=pltpu.SMEM)] + [vmem] * (1 + len(bases)),
+        out_specs=vmem,
+        scratch_shapes=[
+            pltpu.VMEM((6 * high, 8 * LANES), jnp.bfloat16),
+            pltpu.VMEM((WIDE, 8 * LANES), jnp.bfloat16),
+        ],
+        cost_estimate=pl.CostEstimate(
+            flops=12 * high * 8 * LANES * WIDE, bytes_accessed=2000000, transcendentals=0
+        ),
+        compiler_params=pltpu.CompilerParams(vmem_limit_bytes=16 * 1024 * 1024),
+    )(column, source, *bases)
+
+
+def total_kernel(groups, group_ref, *refs):
+    partials = refs[:groups]
+    grad_ref, part_ref, sum_ref = refs[groups:]
+    per_owner = ND_DEV // WIDE
+    high = groups * per_owner
+    total = partials[0][...]
+    for partial in partials[1:]:
+        total = total + partial[...]
+    sum_ref[...] = total
+    design = total[: 3 * high]
+    squares = jnp.sum(design * design)
+    spent = jnp.sum(total[3 * high : 3 * high + 1])
     lane = lax.broadcasted_iota(jnp.int32, (1, LANES), 1)
     stats = jnp.where(lane == 0, squares, jnp.where(lane == 1, spent, 0.0))
     part_ref[...] = jnp.broadcast_to(stats[None], part_ref.shape)
-
-
-def assembled(place, arrays, columns):
-    groups = len(arrays)
-    high = groups * (ND_DEV // WIDE)
+    for c in range(3):
+        start = pl.multiple_of(c * high + group_ref[0] * per_owner, per_owner)
+        block = sum_ref[pl.ds(start, per_owner), :]
+        for i in range(per_owner):
+            grad_ref[c : c + 1, i * WIDE : (i + 1) * WIDE] = block[i : i + 1, :]
+
+
+def totalled(group, partials, columns):
+    groups = len(partials)
     vmem = pl.BlockSpec(memory_space=pltpu.VMEM)
     return pl.pallas_call(
-        functools.partial(assemble_kernel, groups, columns),
+        functools.partial(total_kernel, groups),
         out_shape=(
             jax.ShapeDtypeStruct((3, ND_DEV), jnp.float32),
             jax.ShapeDtypeStruct((columns, 1, LANES), jnp.float32),
         ),
         in_specs=[pl.BlockSpec(memory_space=pltpu.SMEM)] + [vmem] * groups,
         out_specs=(vmem, vmem),
-        scratch_shapes=[
-            pltpu.VMEM((6 * high, 8 * LANES), jnp.bfloat16),
-            pltpu.VMEM((WIDE, 8 * LANES), jnp.bfloat16),
-            pltpu.VMEM((6 * high, WIDE), jnp.float32),
-        ],
-        compiler_params=pltpu.CompilerParams(vmem_limit_bytes=32 * 1024 * 1024),
-    )(place, *arrays)
+        scratch_shapes=[pltpu.VMEM(partials[0].shape, jnp.float32)],
+        compiler_params=pltpu.CompilerParams(vmem_limit_bytes=4 * 1024 * 1024),
+    )(group, *partials)
 
 
 def scale_kernel(over_nodes, over_elements, grad_ref, part_ref, out_ref, objective_ref):
@@ -314,26 +386,27 @@
         ),
         in_specs=[vmem, vmem],
         out_specs=(vmem, vmem),
+        compiler_params=pltpu.CompilerParams(vmem_limit_bytes=2 * 1024 * 1024),
     )(grad, parts)
-
-
-def shifted(array, axis, by):
-    devices = lax.axis_size(axis)
-    return lax.ppermute(array, axis, [(i, (i + by) % devices) for i in range(devices)])
 
 
 def body(velocity, adjoint, spacing, elem_count, design_map):
     slots = velocity.shape[-1]
     groups = lax.axis_size("grp")
     columns = lax.axis_size(ELEM)
+    group = lax.axis_index("grp").astype(jnp.int32).reshape(1)
+    column = lax.axis_index(ELEM).astype(jnp.int32).reshape(1)
     sent = element_terms(elem_count, velocity, adjoint, spacing, design_map)
-    within = lax.ppermute(sent, "elem_2", [(0, 1), (1, 0)])
     partner = [(e + 1) % columns if e % 2 else (e - 1) % columns for e in range(columns)]
     across = lax.ppermute(sent, ELEM, list(enumerate(partner)))
-    three = jnp.stack([sent, within, across])
-    arrays = [three] + [shifted(three, "grp", by) for by in range(1, groups)]
-    place = jnp.stack([lax.axis_index("grp"), lax.axis_index(ELEM)]).astype(jnp.int32)
-    grad, parts = assembled(place, arrays, columns)
+    within = lax.ppermute(sent, "elem_2", [(0, 1), (1, 0)])
+    partial = spread(column, sent, None, groups, columns)
+    partial = spread(column, within, partial, groups, columns)
+    partial = spread(column, across, partial, groups, columns)
+    partials = [partial] + [
+        lax.ppermute(partial, "grp", [(i, i ^ by) for i in range(groups)]) for by in (1, 3, 2)
+    ]
+    grad, parts = totalled(group, partials, columns)
     parts = lax.all_to_all(parts, ELEM, split_axis=0, concat_axis=0, tiled=True)
     devices = groups * columns
     direction, objective = scaled(

time: 47.3 us -> 36.1 us (0.76)
  Pallas kernels: 10.8 us -> 5.6 us
  local copies, waits for them, and re-layouts: 4.94 us -> 0 us
  starting transfers between devices: 10.7 us -> 7.36 us
  blocking collectives: 14 us -> 16.5 us
    unnamed x12 -> x0, local copies, waits for them, and re-layouts: 4.94 us -> none
    pallas_call x2 -> x5, Pallas kernels: 9.28 us -> 4.88 us  [the longest x1 3.08 us: element_terms(): pl.pallas_call(terms_kernel, out_shape=pltpu.VMEM((SENT, LANES), jnp.floa...]
    all_to_all x1, blocking collectives: 14 us -> 16.5 us  [body(): parts = lax.all_to_all(parts, ELEM, split_axis=0, concat_axis=0, tiled=True)]
    ppermute x1, starting transfers between devices: 3.47 us -> 1.5 us  [body(): within = lax.ppermute(sent, 'elem_2', [(0, 1), (1, 0)])]
    ppermute x1, starting transfers between devices: 2.77 us -> 1.36 us  [body(): across = lax.ppermute(sent, ELEM, list(enumerate(partner)))]
    ppermute x1, waiting for transfers between devices: 0.84 us -> 0.01 us  [body(): within = lax.ppermute(sent, 'elem_2', [(0, 1), (1, 0)])]
    pallas_call x1, Pallas kernels: 1.48 us -> 0.72 us  [scaled(): pl.pallas_call(functools.partial(scale_kernel, over_nodes, over_elements)...]
    ppermute x1, waiting for transfers between devices: 0.01 us -> 0.74 us  [body(): across = lax.ppermute(sent, ELEM, list(enumerate(partner)))]
  transfers between devices with their start and end apart: 5 -> 5, of which waited for: 4 -> 3; matrix products, arithmetic and copies ran while one was open for 0% -> 0% of each run, Pallas kernels for 0% -> 3%
where the time goes in v2:
time: 36.1 us; the launch traced here: 35.9 us
  blocking collectives  16.5 us (46%)
  starting transfers between devices  7.36 us (20%)
  Pallas kernels  5.6 us (16%)
  waiting for transfers between devices  5.08 us (14%)
  between operations  1.33 us (4%)
    all_to_all x1, blocking collectives, body(): parts = lax.all_to_all(parts, ELEM, split_axis=0, concat_axis=0, tiled=True)  16.5 us
    ppermute x3, starting transfers between devices, body(): lax.ppermute(partial, 'grp', [(i, i ^ by) for i in range(groups)])  4.5 us
    ppermute x3, waiting for transfers between devices, body(): lax.ppermute(partial, 'grp', [(i, i ^ by) for i in range(groups)])  4.33 us
    pallas_call x1, Pallas kernels, element_terms(): pl.pallas_call(terms_kernel, out_shape=pltpu.VMEM((SENT, LANES), jnp.floa...  3.08 us
    pallas_call x3, Pallas kernels, spread(): pl.pallas_call(functools.partial(spread_kernel, groups, columns, base is...  1.62 us
    ppermute x1, starting transfers between devices, body(): within = lax.ppermute(sent, 'elem_2', [(0, 1), (1, 0)])  1.5 us
    ppermute x1, starting transfers between devices, body(): across = lax.ppermute(sent, ELEM, list(enumerate(partner)))  1.36 us
    ppermute x1, waiting for transfers between devices, body(): across = lax.ppermute(sent, ELEM, list(enumerate(partner)))  0.74 us
  transfers between devices with their start and end apart: 5, of which 3 were waited for; matrix products, arithmetic and copies ran while one was open for 0% of the time, Pallas kernels for 3%

profile of v2, /device:TPU:1, one launch (start us, length us, event | category | flops | bytes accessed | tf_op | source)
XLA Modules:
  0.0 35.9 jit_solution(6565650853444677969)
XLA Ops:
  1.3 3.1 %shard_map.77.source = f32[40,128]{1,0:T(8,128)S(1)} custom-call(s32[1]{0:T(128)S(6)} %copy.8.count_ref, f32[3,343,128]{2,1,0:T(8,128)} %u_hbm.1, f32[3,343,128]{2,1,0:T(8,128)} %w_hbm.1, f32[3,128]{1,0:T(4,128)} %h_hbm.1, s32[8,128]{1,0:T(8,128)} %map_hbm.1, f32[144,128]{1,0:T(8,128)} %constant.21.clone.tab_hbm), custom_call_target="tpu_custom_call" | custom-call | tf_op jit(solution)/shard_map/pallas_call | solution.py:250
  4.4 1.5 %collective-permute-start.1 = (f32[40,128]{1,0:T(8,128)S(1)}, f32[40,128]{1,0:T(8,128)S(1)}, u32[]{:S(2)}, u32[]{:S(2)}) collective-permute-start(f32[40,128]{1,0:T(8,128)S(1)} %shard_map.77.source), channel_id=1, source_target_pairs={{0,1},{1,0},{2,3},{3,2},{4,5},{5,4},{6,7},{7,6},{8,9},{9,8},{10,11... | collective-permute-start | bytes 61448 | tf_op jit(solution)/shard_map/ppermute | solution.py:402
  5.9 1.4 %collective-permute-start = (f32[40,128]{1,0:T(8,128)S(1)}, f32[40,128]{1,0:T(8,128)S(1)}, u32[]{:S(2)}, u32[]{:S(2)}) collective-permute-start(f32[40,128]{1,0:T(8,128)S(1)} %shard_map.77.source), channel_id=1, source_target_pairs={{0,31},{1,2},{2,1},{3,4},{4,3},{5,6},{6,5},{7,8},{8,7},{9,10},{10,... | collective-permute-start | bytes 61448 | tf_op jit(solution)/shard_map/ppermute | solution.py:401
  7.2 0.5 %shard_map.78.refs_0_ = f32[104,256]{1,0:T(8,128)S(1)} custom-call(s32[1]{0:T(128)} %bitcast.1.column_ref, f32[40,128]{1,0:T(8,128)S(1)} %shard_map.77.source), custom_call_target="tpu_custom_call" | custom-call | flops 100663296 | bytes 2000000 | tf_op jit(solution)/shard_map/pallas_call | solution.py:316
  7.8 0.0 collective-permute-done.1.source
  7.8 0.5 %shard_map.79.refs_0_ = f32[104,256]{1,0:T(8,128)S(1)} custom-call(s32[1]{0:T(128)} %bitcast.1.column_ref, f32[40,128]{1,0:T(8,128)S(1)} %collective-permute-done.1.source, f32[104,256]{1,0:T(8,128)S(1)} %shard_map.78.refs_0_), custom_call_target="tpu_custom_call" | custom-call | flops 100663296 | bytes 2000000 | tf_op jit(solution)/shard_map/pallas_call | solution.py:316
  8.3 0.7 %collective-permute-done.source = f32[40,128]{1,0:T(8,128)S(1)} collective-permute-done((f32[40,128]{1,0:T(8,128)S(1)}, f32[40,128]{1,0:T(8,128)S(1)}, u32[]{:S(2)}, u32[]{:S(2)}) %collective-permute-start) | collective-permute-done | bytes 20512 | tf_op jit(solution)/shard_map/ppermute | solution.py:401
  9.1 0.5 %shard_map.80.refs_0_ = f32[104,256]{1,0:T(8,128)S(1)} custom-call(s32[1]{0:T(128)} %bitcast.1.column_ref, f32[40,128]{1,0:T(8,128)S(1)} %collective-permute-done.source, f32[104,256]{1,0:T(8,128)S(1)} %shard_map.79.refs_0_), custom_call_target="tpu_custom_call" | custom-call | flops 100663296 | bytes 2000000 | tf_op jit(solution)/shard_map/pallas_call | solution.py:316
  9.6 3.8 %collective-permute-start.4 = (f32[104,256]{1,0:T(8,128)S(1)}, f32[104,256]{1,0:T(8,128)S(1)}, u32[]{:S(2)}, u32[]{:S(2)}) collective-permute-start(f32[104,256]{1,0:T(8,128)S(1)} %shard_map.80.refs_0_), channel_id=1, source_target_pairs={{0,64},{32,96},{64,0},{96,32},{1,65},{33,97},{65,1},{97,33},{2,66}... | collective-permute-start | bytes 319496 | tf_op jit(solution)/shard_map/ppermute | solution.py:407
  13.4 0.4 %collective-permute-start.3 = (f32[104,256]{1,0:T(8,128)S(1)}, f32[104,256]{1,0:T(8,128)S(1)}, u32[]{:S(2)}, u32[]{:S(2)}) collective-permute-start(f32[104,256]{1,0:T(8,128)S(1)} %shard_map.80.refs_0_), channel_id=1, source_target_pairs={{0,96},{32,64},{64,32},{96,0},{1,97},{33,65},{65,33},{97,1},{2,98}... | collective-permute-start | bytes 319496 | tf_op jit(solution)/shard_map/ppermute | solution.py:407
  13.8 0.3 collective-permute-start.2
  14.1 1.4 %collective-permute-done.4.refs_3_ = f32[104,256]{1,0:T(8,128)S(1)} collective-permute-done((f32[104,256]{1,0:T(8,128)S(1)}, f32[104,256]{1,0:T(8,128)S(1)}, u32[]{:S(2)}, u32[]{:S(2)}) %collective-permute-start.4) | collective-permute-done | bytes 106528 | tf_op jit(solution)/shard_map/ppermute | solution.py:407
  15.5 3.0 %collective-permute-done.3.refs_2_ = f32[104,256]{1,0:T(8,128)S(1)} collective-permute-done((f32[104,256]{1,0:T(8,128)S(1)}, f32[104,256]{1,0:T(8,128)S(1)}, u32[]{:S(2)}, u32[]{:S(2)}) %collective-permute-start.3) | collective-permute-done | bytes 106528 | tf_op jit(solution)/shard_map/ppermute | solution.py:407
  18.5 0.0 collective-permute-done.2.refs_1_
  18.5 0.2 shard_map.81
  18.6 16.5 %all_to_all.5.part_ref = f32[32,1,128]{2,1,0:T(1,128)S(1)} all-to-all(f32[32,1,128]{2,1,0:T(1,128)S(1)} %get-tuple-element.7), channel_id=1, replica_groups=mesh['grp'=4,'elem_0'=4,'elem_1'=4,'elem_2'=2] {'elem_0','elem_1','elem_2'}, dimensions={0} | all-to-all | bytes 32768 | tf_op jit(solution)/shard_map/all_to_all | solution.py:410
  35.2 0.7 %shard_map.82 = (f32[3,2048]{1,0:T(4,128)}, f32[1,1]{1,0:T(1,128)}) custom-call(f32[3,2048]{1,0:T(4,128)S(1)} %get-tuple-element.6.grad_ref, f32[32,1,128]{2,1,0:T(1,128)S(1)} %all_to_all.5.part_ref), custom_call_target="tpu_custom_call" | custom-call | tf_op jit(solution)/shard_map/pallas_call | solution.py:381
Async XLA Ops:
  4.4 3.4 %collective-permute-start.1 = (f32[40,128]{1,0:T(8,128)S(1)}, f32[40,128]{1,0:T(8,128)S(1)}, u32[]{:S(2)}, u32[]{:S(2)}) collective-permute-start(f32[40,128]{1,0:T(8,128)S(1)} %shard_map.77.source), channel_id=1, source_target_pairs={{0,1},{1,0},{2,3},{3,2},{4,5},{5,4},{6,7},{7,6},{8,9},{9,8},{10,11... | collective-permute-start | bytes 61448 | tf_op jit(solution)/shard_map/ppermute | solution.py:402
  5.9 3.2 %collective-permute-start = (f32[40,128]{1,0:T(8,128)S(1)}, f32[40,128]{1,0:T(8,128)S(1)}, u32[]{:S(2)}, u32[]{:S(2)}) collective-permute-start(f32[40,128]{1,0:T(8,128)S(1)} %shard_map.77.source), channel_id=1, source_target_pairs={{0,31},{1,2},{2,1},{3,4},{4,3},{5,6},{6,5},{7,8},{8,7},{9,10},{10,... | collective-permute-start | bytes 61448 | tf_op jit(solution)/shard_map/ppermute | solution.py:401
  9.6 5.9 %collective-permute-start.4 = (f32[104,256]{1,0:T(8,128)S(1)}, f32[104,256]{1,0:T(8,128)S(1)}, u32[]{:S(2)}, u32[]{:S(2)}) collective-permute-start(f32[104,256]{1,0:T(8,128)S(1)} %shard_map.80.refs_0_), channel_id=1, source_target_pairs={{0,64},{32,96},{64,0},{96,32},{1,65},{33,97},{65,1},{97,33},{2,66}... | collective-permute-start | bytes 319496 | tf_op jit(solution)/shard_map/ppermute | solution.py:407
  13.4 5.1 %collective-permute-start.3 = (f32[104,256]{1,0:T(8,128)S(1)}, f32[104,256]{1,0:T(8,128)S(1)}, u32[]{:S(2)}, u32[]{:S(2)}) collective-permute-start(f32[104,256]{1,0:T(8,128)S(1)} %shard_map.80.refs_0_), channel_id=1, source_target_pairs={{0,96},{32,64},{64,32},{96,0},{1,97},{33,65},{65,33},{97,1},{2,98}... | collective-permute-start | bytes 319496 | tf_op jit(solution)/shard_map/ppermute | solution.py:407
  13.8 4.6 %collective-permute-start.2 = (f32[104,256]{1,0:T(8,128)S(1)}, f32[104,256]{1,0:T(8,128)S(1)}, u32[]{:S(2)}, u32[]{:S(2)}) collective-permute-start(f32[104,256]{1,0:T(8,128)S(1)} %shard_map.80.refs_0_), channel_id=1, source_target_pairs={{0,32},{32,0},{64,96},{96,64},{1,33},{33,1},{65,97},{97,65},{2,34}... | collective-permute-start | bytes 319496 | tf_op jit(solution)/shard_map/ppermute | solution.py:407

commit v3 on v2

--- a/solution.py
+++ b/solution.py
@@ -17,6 +17,13 @@
 GRP_ELEM = ("grp", "elem_0", "elem_1", "elem_2")
 SENT = 40
 WIDE = 256
+UNROLL = 1
+PITCH = 9
+
+
+def log2(number):
+    assert number & (number - 1) == 0
+    return number.bit_length() - 1
 
 
 def lobatto(degree):
@@ -108,19 +115,15 @@
     tab_ref,
     ga_ref,
     gb_ref,
+    gc_ref,
     mom_ref,
     sems,
 ):
     n = P_SIZE
     fields = [(ref, i) for ref in (u_ref, w_ref) for i in range(3)]
     rows = pl.ds(0, n)
-    pairs = (
-        (u_hbm, u_ref),
-        (w_hbm, w_ref),
-        (tab_hbm, tab_ref),
-        (h_hbm, h_ref),
-        (map_hbm, map_ref),
-    )
+    pairs = [(source.at[i], ref.at[i]) for source, ref in ((u_hbm, u_ref), (w_hbm, w_ref)) for i in range(3)]
+    pairs += [(tab_hbm, tab_ref), (h_hbm, h_ref), (map_hbm, map_ref)]
     copies = [
         pltpu.make_async_copy(source, target, sems.at[i])
         for i, (source, target) in enumerate(pairs)
@@ -133,20 +136,16 @@
         for a, value in enumerate(along_vectors(slabs)):
             ga_ref[f, a, b, rows, :] = value
 
-    def half(start):
-        def step(b, carry):
-            for f in range(start, start + 3):
-                first(f, *fields[f], b)
+    mom_ref[...] = jnp.zeros_like(mom_ref)
+    for f, (ref, i) in enumerate(fields):
+        copies[f].wait()
+
+        def step(b, carry, f=f, ref=ref, i=i):
+            first(f, ref, i, b)
             return carry
 
-        lax.fori_loop(0, n, step, 0)
-
-    mom_ref[...] = jnp.zeros_like(mom_ref)
-    copies[0].wait()
-    half(0)
-    copies[1].wait()
-    half(3)
-    for copy in copies[2:]:
+        lax.fori_loop(0, n, step, 0, unroll=UNROLL)
+    for copy in copies[6:]:
         copy.wait()
 
     h = h_ref[...]
@@ -159,16 +158,15 @@
             slabs = [ref[i, pl.ds(base + b * n, n), :] for b in range(n)]
             for b, value in enumerate(along_vectors(slabs)):
                 gb_ref[f, b, rows, :] = value
+            slabs = [ref[i, pl.ds(base + c, n, stride=n), :] for c in range(n)]
+            for c, value in enumerate(along_vectors(slabs)):
+                gc_ref[pl.ds((f * n + c) * PITCH, n), :] = value
         sums = [[None, None] for _ in range(6)]
         spent = None
         for b in range(n):
             grads = []
-            for f, (ref, i) in enumerate(fields):
-                gc = None
-                for c in range(n):
-                    row = ref[i, pl.ds(base + b * n + c, 1), :]
-                    piece = tab_ref[pl.ds(COLUMN + 8 * c, n), :] * row
-                    gc = piece if gc is None else gc + piece
+            for f in range(6):
+                gc = gc_ref[pl.ds(f * n * PITCH + b, n, stride=PITCH), :]
                 grads.append([ga_ref[f, a, b, rows, :], gb_ref[f, b, rows, :], gc])
             gu, gw = grads[:3], grads[3:]
 
@@ -261,8 +259,9 @@
             pltpu.VMEM((TABLE_ROWS, LANES), jnp.float32),
             pltpu.VMEM((6, P_SIZE, P_SIZE, 8, LANES), jnp.float32),
             pltpu.VMEM((6, P_SIZE, 8, LANES), jnp.float32),
+            pltpu.VMEM((6 * P_SIZE * PITCH, LANES), jnp.float32),
             pltpu.VMEM((25, 8, LANES), jnp.float32),
-            pltpu.SemaphoreType.DMA((5,)),
+            pltpu.SemaphoreType.DMA((9,)),
         ],
         compiler_params=pltpu.CompilerParams(vmem_limit_bytes=16 * 1024 * 1024),
     )(count, *arrays)
@@ -274,24 +273,39 @@
     column = column_ref[0]
     per_owner = ND_DEV // WIDE
     high = groups * per_owner
-    iota_wide = lax.broadcasted_iota(jnp.int32, (WIDE, LANES), 0)
-    iota_high = lax.broadcasted_iota(jnp.int32, (high, LANES), 0)
+    half = jnp.bfloat16
+    tile = (16, LANES)
+
+    def rows_from(count):
+        ramp = lax.broadcasted_iota(jnp.int32, (count, LANES), 0).astype(jnp.float32)
+        return ramp.astype(half).reshape(count // 16, *tile)
+
+    def spread_row(rows, k):
+        return jnp.broadcast_to(rows[k : k + 1], tile).astype(half)[None]
+
+    ramp_wide = rows_from(WIDE)
+    ramp_high = rows_from(high)
+    node = source[pl.ds(24, 8), :].astype(jnp.int32)
+    owner = node >> log2(ND_DEV)
+    at = (owner >> log2(columns)) * per_owner + ((node & (ND_DEV - 1)) >> log2(WIDE))
+    at = jnp.where((owner & (columns - 1)) == column, at, -1).astype(jnp.float32)
+    low = (node & (WIDE - 1)).astype(jnp.float32)
+    parts = []
+    for c in range(3):
+        value = source[pl.ds(8 * c, 8), :]
+        coarse = value.astype(half).astype(jnp.float32)
+        parts.append((coarse, value - coarse))
+    one = jnp.ones((), half)
+    zero = jnp.zeros((), half)
     for k in range(8):
-        node = source[pl.ds(24 + k, 1), :].astype(jnp.int32)
-        owner = node // ND_DEV
-        mine = owner % columns == column
-        low = node % WIDE
-        at = (owner // columns) * per_owner + (node % ND_DEV) // WIDE
-        at = jnp.where(mine, at, -1)
         lanes = pl.ds(k * LANES, LANES)
-        right_ref[:, lanes] = jnp.where(iota_wide == low, 1.0, 0.0).astype(jnp.bfloat16)
-        hit = iota_high == at
+        mask = jnp.where(ramp_wide == spread_row(low, k), one, zero)
+        right_ref[:, lanes] = mask.reshape(WIDE, LANES)
+        hit = ramp_high == spread_row(at, k)
         for c in range(3):
-            value = source[pl.ds(8 * c + k, 1), :]
-            coarse = value.astype(jnp.bfloat16).astype(jnp.float32)
-            for piece, part in enumerate((coarse, value - coarse)):
-                row = (piece * 3 + c) * high
-                left_ref[pl.ds(row, high), lanes] = jnp.where(hit, part, 0.0).astype(jnp.bfloat16)
+            for piece in range(2):
+                placed = jnp.where(hit, spread_row(parts[c][piece], k), zero)
+                left_ref[pl.ds((piece * 3 + c) * high, high), lanes] = placed.reshape(high, LANES)
     both = lax.dot_general(
         left_ref[...],
         right_ref[...],
@@ -398,8 +412,8 @@
     column = lax.axis_index(ELEM).astype(jnp.int32).reshape(1)
     sent = element_terms(elem_count, velocity, adjoint, spacing, design_map)
     partner = [(e + 1) % columns if e % 2 else (e - 1) % columns for e in range(columns)]
+    within = lax.ppermute(sent, "elem_2", [(0, 1), (1, 0)])
     across = lax.ppermute(sent, ELEM, list(enumerate(partner)))
-    within = lax.ppermute(sent, "elem_2", [(0, 1), (1, 0)])
     partial = spread(column, sent, None, groups, columns)
     partial = spread(column, within, partial, groups, columns)
     partial = spread(column, across, partial, groups, columns)

time: 36.1 us -> 35.7 us (0.989)
  Pallas kernels: 5.6 us -> 4.98 us
    pallas_call x3, Pallas kernels: 1.62 us -> 1.18 us  [spread(): pl.pallas_call(functools.partial(spread_kernel, groups, columns, base is...]
  transfers between devices with their start and end apart: 5 -> 5, of which waited for: 3 -> 3; matrix products, arithmetic and copies ran while one was open for 0% -> 0% of each run, Pallas kernels for 3% -> 2%
where the time goes in v3:
time: 35.7 us; the launch traced here: 35.5 us
  blocking collectives  16.5 us (46%)
  starting transfers between devices  7.36 us (21%)
  waiting for transfers between devices  5.38 us (15%)
  Pallas kernels  4.98 us (14%)
  between operations  1.33 us (4%)
    all_to_all x1, blocking collectives, body(): parts = lax.all_to_all(parts, ELEM, split_axis=0, concat_axis=0, tiled=True)  16.5 us
    ppermute x3, starting transfers between devices, body(): lax.ppermute(partial, 'grp', [(i, i ^ by) for i in range(groups)])  4.5 us
    ppermute x3, waiting for transfers between devices, body(): lax.ppermute(partial, 'grp', [(i, i ^ by) for i in range(groups)])  4.33 us
    pallas_call x1, Pallas kernels, element_terms(): pl.pallas_call(terms_kernel, out_shape=pltpu.VMEM((SENT, LANES), jnp.floa...  2.9 us
    ppermute x1, starting transfers between devices, body(): within = lax.ppermute(sent, 'elem_2', [(0, 1), (1, 0)])  1.5 us
    ppermute x1, starting transfers between devices, body(): across = lax.ppermute(sent, ELEM, list(enumerate(partner)))  1.36 us
    pallas_call x3, Pallas kernels, spread(): pl.pallas_call(functools.partial(spread_kernel, groups, columns, base is...  1.18 us
    ppermute x1, waiting for transfers between devices, body(): across = lax.ppermute(sent, ELEM, list(enumerate(partner)))  1.04 us
  transfers between devices with their start and end apart: 5, of which 3 were waited for; matrix products, arithmetic and copies ran while one was open for 0% of the time, Pallas kernels for 2%

profile of v3, /device:TPU:1, one launch (start us, length us, event | category | flops | bytes accessed | tf_op | source)
XLA Modules:
  0.0 35.5 jit_solution(9151172208068689913)
XLA Ops:
  1.3 2.9 %shard_map.77.source = f32[40,128]{1,0:T(8,128)S(1)} custom-call(s32[1]{0:T(128)S(6)} %copy.8.count_ref, f32[3,343,128]{2,1,0:T(8,128)} %u_hbm.1, f32[3,343,128]{2,1,0:T(8,128)} %w_hbm.1, f32[3,128]{1,0:T(4,128)} %h_hbm.1, s32[8,128]{1,0:T(8,128)} %map_hbm.1, f32[144,128]{1,0:T(8,128)} %constant.21.clone.tab_hbm), custom_call_target="tpu_custom_call" | custom-call | tf_op jit(solution)/shard_map/pallas_call | solution.py:248
  4.2 1.5 %collective-permute-start.1 = (f32[40,128]{1,0:T(8,128)S(1)}, f32[40,128]{1,0:T(8,128)S(1)}, u32[]{:S(2)}, u32[]{:S(2)}) collective-permute-start(f32[40,128]{1,0:T(8,128)S(1)} %shard_map.77.source), channel_id=1, source_target_pairs={{0,1},{1,0},{2,3},{3,2},{4,5},{5,4},{6,7},{7,6},{8,9},{9,8},{10,11... | collective-permute-start | bytes 61448 | tf_op jit(solution)/shard_map/ppermute | solution.py:415
  5.7 1.4 %collective-permute-start = (f32[40,128]{1,0:T(8,128)S(1)}, f32[40,128]{1,0:T(8,128)S(1)}, u32[]{:S(2)}, u32[]{:S(2)}) collective-permute-start(f32[40,128]{1,0:T(8,128)S(1)} %shard_map.77.source), channel_id=1, source_target_pairs={{0,31},{1,2},{2,1},{3,4},{4,3},{5,6},{6,5},{7,8},{8,7},{9,10},{10,... | collective-permute-start | bytes 61448 | tf_op jit(solution)/shard_map/ppermute | solution.py:416
  7.0 0.4 %shard_map.78.refs_0_ = f32[104,256]{1,0:T(8,128)S(1)} custom-call(s32[1]{0:T(128)} %bitcast.1.column_ref, f32[40,128]{1,0:T(8,128)S(1)} %shard_map.77.source), custom_call_target="tpu_custom_call" | custom-call | flops 100663296 | bytes 2000000 | tf_op jit(solution)/shard_map/pallas_call | solution.py:330
  7.4 0.0 collective-permute-done.1.source
  7.4 0.4 %shard_map.79.refs_0_ = f32[104,256]{1,0:T(8,128)S(1)} custom-call(s32[1]{0:T(128)} %bitcast.1.column_ref, f32[40,128]{1,0:T(8,128)S(1)} %collective-permute-done.1.source, f32[104,256]{1,0:T(8,128)S(1)} %shard_map.78.refs_0_), custom_call_target="tpu_custom_call" | custom-call | flops 100663296 | bytes 2000000 | tf_op jit(solution)/shard_map/pallas_call | solution.py:330
  7.9 1.0 %collective-permute-done.source = f32[40,128]{1,0:T(8,128)S(1)} collective-permute-done((f32[40,128]{1,0:T(8,128)S(1)}, f32[40,128]{1,0:T(8,128)S(1)}, u32[]{:S(2)}, u32[]{:S(2)}) %collective-permute-start) | collective-permute-done | bytes 20512 | tf_op jit(solution)/shard_map/ppermute | solution.py:416
  8.9 0.4 %shard_map.80.refs_0_ = f32[104,256]{1,0:T(8,128)S(1)} custom-call(s32[1]{0:T(128)} %bitcast.1.column_ref, f32[40,128]{1,0:T(8,128)S(1)} %collective-permute-done.source, f32[104,256]{1,0:T(8,128)S(1)} %shard_map.79.refs_0_), custom_call_target="tpu_custom_call" | custom-call | flops 100663296 | bytes 2000000 | tf_op jit(solution)/shard_map/pallas_call | solution.py:330
  9.3 3.8 %collective-permute-start.4 = (f32[104,256]{1,0:T(8,128)S(1)}, f32[104,256]{1,0:T(8,128)S(1)}, u32[]{:S(2)}, u32[]{:S(2)}) collective-permute-start(f32[104,256]{1,0:T(8,128)S(1)} %shard_map.80.refs_0_), channel_id=1, source_target_pairs={{0,64},{32,96},{64,0},{96,32},{1,65},{33,97},{65,1},{97,33},{2,66}... | collective-permute-start | bytes 319496 | tf_op jit(solution)/shard_map/ppermute | solution.py:421
  13.1 0.4 %collective-permute-start.3 = (f32[104,256]{1,0:T(8,128)S(1)}, f32[104,256]{1,0:T(8,128)S(1)}, u32[]{:S(2)}, u32[]{:S(2)}) collective-permute-start(f32[104,256]{1,0:T(8,128)S(1)} %shard_map.80.refs_0_), channel_id=1, source_target_pairs={{0,96},{32,64},{64,32},{96,0},{1,97},{33,65},{65,33},{97,1},{2,98}... | collective-permute-start | bytes 319496 | tf_op jit(solution)/shard_map/ppermute | solution.py:421
  13.5 0.3 collective-permute-start.2
  13.8 1.4 %collective-permute-done.4.refs_3_ = f32[104,256]{1,0:T(8,128)S(1)} collective-permute-done((f32[104,256]{1,0:T(8,128)S(1)}, f32[104,256]{1,0:T(8,128)S(1)}, u32[]{:S(2)}, u32[]{:S(2)}) %collective-permute-start.4) | collective-permute-done | bytes 106528 | tf_op jit(solution)/shard_map/ppermute | solution.py:421
  15.1 3.0 %collective-permute-done.3.refs_2_ = f32[104,256]{1,0:T(8,128)S(1)} collective-permute-done((f32[104,256]{1,0:T(8,128)S(1)}, f32[104,256]{1,0:T(8,128)S(1)}, u32[]{:S(2)}, u32[]{:S(2)}) %collective-permute-start.3) | collective-permute-done | bytes 106528 | tf_op jit(solution)/shard_map/ppermute | solution.py:421
  18.1 0.0 collective-permute-done.2.refs_1_
  18.1 0.2 shard_map.81
  18.3 16.5 %all_to_all.5.part_ref = f32[32,1,128]{2,1,0:T(1,128)S(1)} all-to-all(f32[32,1,128]{2,1,0:T(1,128)S(1)} %get-tuple-element.7), channel_id=1, replica_groups=mesh['grp'=4,'elem_0'=4,'elem_1'=4,'elem_2'=2] {'elem_0','elem_1','elem_2'}, dimensions={0} | all-to-all | bytes 32768 | tf_op jit(solution)/shard_map/all_to_all | solution.py:424
  34.8 0.7 %shard_map.82 = (f32[3,2048]{1,0:T(4,128)}, f32[1,1]{1,0:T(1,128)}) custom-call(f32[3,2048]{1,0:T(4,128)S(1)} %get-tuple-element.6.grad_ref, f32[32,1,128]{2,1,0:T(1,128)S(1)} %all_to_all.5.part_ref), custom_call_target="tpu_custom_call" | custom-call | tf_op jit(solution)/shard_map/pallas_call | solution.py:395
Async XLA Ops:
  4.2 3.3 %collective-permute-start.1 = (f32[40,128]{1,0:T(8,128)S(1)}, f32[40,128]{1,0:T(8,128)S(1)}, u32[]{:S(2)}, u32[]{:S(2)}) collective-permute-start(f32[40,128]{1,0:T(8,128)S(1)} %shard_map.77.source), channel_id=1, source_target_pairs={{0,1},{1,0},{2,3},{3,2},{4,5},{5,4},{6,7},{7,6},{8,9},{9,8},{10,11... | collective-permute-start | bytes 61448 | tf_op jit(solution)/shard_map/ppermute | solution.py:415
  5.7 3.2 %collective-permute-start = (f32[40,128]{1,0:T(8,128)S(1)}, f32[40,128]{1,0:T(8,128)S(1)}, u32[]{:S(2)}, u32[]{:S(2)}) collective-permute-start(f32[40,128]{1,0:T(8,128)S(1)} %shard_map.77.source), channel_id=1, source_target_pairs={{0,31},{1,2},{2,1},{3,4},{4,3},{5,6},{6,5},{7,8},{8,7},{9,10},{10,... | collective-permute-start | bytes 61448 | tf_op jit(solution)/shard_map/ppermute | solution.py:416
  9.3 5.9 %collective-permute-start.4 = (f32[104,256]{1,0:T(8,128)S(1)}, f32[104,256]{1,0:T(8,128)S(1)}, u32[]{:S(2)}, u32[]{:S(2)}) collective-permute-start(f32[104,256]{1,0:T(8,128)S(1)} %shard_map.80.refs_0_), channel_id=1, source_target_pairs={{0,64},{32,96},{64,0},{96,32},{1,65},{33,97},{65,1},{97,33},{2,66}... | collective-permute-start | bytes 319496 | tf_op jit(solution)/shard_map/ppermute | solution.py:421
  13.1 5.1 %collective-permute-start.3 = (f32[104,256]{1,0:T(8,128)S(1)}, f32[104,256]{1,0:T(8,128)S(1)}, u32[]{:S(2)}, u32[]{:S(2)}) collective-permute-start(f32[104,256]{1,0:T(8,128)S(1)} %shard_map.80.refs_0_), channel_id=1, source_target_pairs={{0,96},{32,64},{64,32},{96,0},{1,97},{33,65},{65,33},{97,1},{2,98}... | collective-permute-start | bytes 319496 | tf_op jit(solution)/shard_map/ppermute | solution.py:421
  13.5 4.6 %collective-permute-start.2 = (f32[104,256]{1,0:T(8,128)S(1)}, f32[104,256]{1,0:T(8,128)S(1)}, u32[]{:S(2)}, u32[]{:S(2)}) collective-permute-start(f32[104,256]{1,0:T(8,128)S(1)} %shard_map.80.refs_0_), channel_id=1, source_target_pairs={{0,32},{32,0},{64,96},{96,64},{1,33},{33,1},{65,97},{97,65},{2,34}... | collective-permute-start | bytes 319496 | tf_op jit(solution)/shard_map/ppermute | solution.py:421

commit v4 on v3

--- a/solution.py
+++ b/solution.py
@@ -16,7 +16,7 @@
 ELEM = ("elem_0", "elem_1", "elem_2")
 GRP_ELEM = ("grp", "elem_0", "elem_1", "elem_2")
 SENT = 40
-WIDE = 256
+WIDE = 128
 UNROLL = 1
 PITCH = 9
 
@@ -58,14 +58,12 @@
 
 
 POINTS, WEIGHTS, DERIVATIVE = one_dimensional()
-COLUMN, ACROSS, ALONG, SIGNS = 0, 56, 72, 88
-TABLE_ROWS = 144
+ACROSS, ALONG, SIGNS = 0, 16, 32
+TABLE_ROWS = 88
 
 
 def table():
     rows = np.zeros((TABLE_ROWS, LANES), np.float32)
-    for c in range(P_SIZE):
-        rows[COLUMN + 8 * c : COLUMN + 8 * c + P_SIZE] = DERIVATIVE[:, c][:, None]
     rows[ACROSS : ACROSS + P_SIZE] = WEIGHTS[:, None]
     rows[ACROSS + 8 : ACROSS + 8 + P_SIZE] = (WEIGHTS * POINTS)[:, None]
     rows[ALONG : ALONG + P_SIZE] = WEIGHTS[:, None]
@@ -162,8 +160,9 @@
             for c, value in enumerate(along_vectors(slabs)):
                 gc_ref[pl.ds((f * n + c) * PITCH, n), :] = value
         sums = [[None, None] for _ in range(6)]
+        kept = [None] * 6
         spent = None
-        for b in range(n):
+        for b in [0, 6, 1, 5, 2, 4, 3]:
             grads = []
             for f in range(6):
                 gc = gc_ref[pl.ds(f * n * PITCH + b, n, stride=PITCH), :]
@@ -177,15 +176,18 @@
             pairs += [cross(c, j) + cross(j, c) for c, j in ((0, 1), (0, 2), (1, 2))]
             own = [gu[0][j] * gu[0][j] + gu[1][j] * gu[1][j] + gu[2][j] * gu[2][j] for j in range(3)]
             squared = own[0] * square[0] + own[1] * square[1] + own[2] * square[2]
-            weight = float(WEIGHTS[b])
-            slope = float(WEIGHTS[b] * POINTS[b])
             for s, value in enumerate(pairs):
-                piece = weight * value
-                sums[s][0] = piece if sums[s][0] is None else sums[s][0] + piece
-                if b != n // 2:
-                    piece = slope * value
-                    sums[s][1] = piece if sums[s][1] is None else sums[s][1] + piece
-            piece = weight * squared
+                if b < n // 2:
+                    kept[s] = value
+                    continue
+                if b == n // 2:
+                    sums[s][0] = sums[s][0] + float(WEIGHTS[b]) * value
+                    continue
+                total = float(WEIGHTS[b]) * (value + kept[s])
+                slope = float(WEIGHTS[b] * POINTS[b]) * (value - kept[s])
+                sums[s][0] = total if sums[s][0] is None else sums[s][0] + total
+                sums[s][1] = slope if sums[s][1] is None else sums[s][1] + slope
+            piece = float(WEIGHTS[b]) * squared
             spent = piece if spent is None else spent + piece
         wa = tab_ref[pl.ds(ALONG + a, 1), :]
         wxa = tab_ref[pl.ds(ALONG + 8 + a, 1), :]
@@ -197,7 +199,7 @@
         mom_ref[24, rows, :] = mom_ref[24, rows, :] + wa * spent
         return carry
 
-    lax.fori_loop(0, n, second, 0)
+    lax.fori_loop(0, n, second, 0, unroll=n)
 
     jacobian = h[0:1] * h[1:2] * h[2:3] * 0.125
     lanes = lax.broadcasted_iota(jnp.int32, (1, LANES), 1)
@@ -267,8 +269,10 @@
     )(count, *arrays)
 
 
-def spread_kernel(groups, columns, adds, column_ref, source, *refs):
-    base_ref = refs[0] if adds else None
+def spread_kernel(groups, columns, count, column_ref, *refs):
+    sources = refs[:count]
+    adds = len(refs) > count + 3
+    base_ref = refs[count]
     sum_ref, left_ref, right_ref = refs[-3:]
     column = column_ref[0]
     per_owner = ND_DEV // WIDE
@@ -285,27 +289,28 @@
 
     ramp_wide = rows_from(WIDE)
     ramp_high = rows_from(high)
-    node = source[pl.ds(24, 8), :].astype(jnp.int32)
-    owner = node >> log2(ND_DEV)
-    at = (owner >> log2(columns)) * per_owner + ((node & (ND_DEV - 1)) >> log2(WIDE))
-    at = jnp.where((owner & (columns - 1)) == column, at, -1).astype(jnp.float32)
-    low = (node & (WIDE - 1)).astype(jnp.float32)
-    parts = []
-    for c in range(3):
-        value = source[pl.ds(8 * c, 8), :]
-        coarse = value.astype(half).astype(jnp.float32)
-        parts.append((coarse, value - coarse))
     one = jnp.ones((), half)
     zero = jnp.zeros((), half)
-    for k in range(8):
-        lanes = pl.ds(k * LANES, LANES)
-        mask = jnp.where(ramp_wide == spread_row(low, k), one, zero)
-        right_ref[:, lanes] = mask.reshape(WIDE, LANES)
-        hit = ramp_high == spread_row(at, k)
+    for s, source in enumerate(sources):
+        node = source[pl.ds(24, 8), :].astype(jnp.int32)
+        owner = node >> log2(ND_DEV)
+        at = (owner >> log2(columns)) * per_owner + ((node & (ND_DEV - 1)) >> log2(WIDE))
+        at = jnp.where((owner & (columns - 1)) == column, at, -1).astype(jnp.float32)
+        low = (node & (WIDE - 1)).astype(jnp.float32)
+        parts = []
         for c in range(3):
-            for piece in range(2):
-                placed = jnp.where(hit, spread_row(parts[c][piece], k), zero)
-                left_ref[pl.ds((piece * 3 + c) * high, high), lanes] = placed.reshape(high, LANES)
+            value = source[pl.ds(8 * c, 8), :]
+            coarse = value.astype(half).astype(jnp.float32)
+            parts.append((coarse, value - coarse))
+        for k in range(8):
+            lanes = pl.ds((8 * s + k) * LANES, LANES)
+            mask = jnp.where(ramp_wide == spread_row(low, k), one, zero)
+            right_ref[:, lanes] = mask.reshape(WIDE, LANES)
+            hit = ramp_high == spread_row(at, k)
+            for c in range(3):
+                for piece in range(2):
+                    placed = jnp.where(hit, spread_row(parts[c][piece], k), zero)
+                    left_ref[pl.ds((piece * 3 + c) * high, high), lanes] = placed.reshape(high, LANES)
     both = lax.dot_general(
         left_ref[...],
         right_ref[...],
@@ -319,28 +324,28 @@
         sum_ref[rest, :] = base_ref[rest, :]
     else:
         sum_ref[pl.ds(0, 3 * high), :] = total
-        sum_ref[rest, 0:LANES] = source[pl.ds(32, 8), :]
-        sum_ref[rest, LANES:WIDE] = jnp.zeros((8, WIDE - LANES), jnp.float32)
-
-
-def spread(column, source, base, groups, columns):
+        sum_ref[rest, 0:LANES] = sources[0][pl.ds(32, 8), :]
+
+
+def spread(column, sources, base, groups, columns):
+    count = len(sources)
     high = groups * (ND_DEV // WIDE)
     vmem = pl.BlockSpec(memory_space=pltpu.VMEM)
     bases = () if base is None else (base,)
     return pl.pallas_call(
-        functools.partial(spread_kernel, groups, columns, base is not None),
+        functools.partial(spread_kernel, groups, columns, count),
         out_shape=jax.ShapeDtypeStruct((3 * high + 8, WIDE), jnp.float32),
-        in_specs=[pl.BlockSpec(memory_space=pltpu.SMEM)] + [vmem] * (1 + len(bases)),
+        in_specs=[pl.BlockSpec(memory_space=pltpu.SMEM)] + [vmem] * (count + len(bases)),
         out_specs=vmem,
         scratch_shapes=[
-            pltpu.VMEM((6 * high, 8 * LANES), jnp.bfloat16),
-            pltpu.VMEM((WIDE, 8 * LANES), jnp.bfloat16),
+            pltpu.VMEM((6 * high, count * 8 * LANES), jnp.bfloat16),
+            pltpu.VMEM((WIDE, count * 8 * LANES), jnp.bfloat16),
         ],
         cost_estimate=pl.CostEstimate(
-            flops=12 * high * 8 * LANES * WIDE, bytes_accessed=2000000, transcendentals=0
+            flops=12 * high * count * 8 * LANES * WIDE, bytes_accessed=2000000, transcendentals=0
         ),
         compiler_params=pltpu.CompilerParams(vmem_limit_bytes=16 * 1024 * 1024),
-    )(column, source, *bases)
+    )(column, *sources, *bases)
 
 
 def total_kernel(groups, group_ref, *refs):
@@ -414,9 +419,8 @@
     partner = [(e + 1) % columns if e % 2 else (e - 1) % columns for e in range(columns)]
     within = lax.ppermute(sent, "elem_2", [(0, 1), (1, 0)])
     across = lax.ppermute(sent, ELEM, list(enumerate(partner)))
-    partial = spread(column, sent, None, groups, columns)
-    partial = spread(column, within, partial, groups, columns)
-    partial = spread(column, across, partial, groups, columns)
+    partial = spread(column, (sent,), None, groups, columns)
+    partial = spread(column, (within, across), partial, groups, columns)
     partials = [partial] + [
         lax.ppermute(partial, "grp", [(i, i ^ by) for i in range(groups)]) for by in (1, 3, 2)
     ]

time: 35.7 us -> 35.2 us (0.986)
  starting transfers between devices: 7.36 us -> 10.6 us
  blocking collectives: 16.5 us -> 13.9 us
  waiting for transfers between devices: 5.38 us -> 4.41 us
    all_to_all x1, blocking collectives: 16.5 us -> 13.9 us  [body(): parts = lax.all_to_all(parts, ELEM, split_axis=0, concat_axis=0, tiled=True)]
    ppermute x1, starting transfers between devices: 1.5 us -> 3.47 us  [body(): within = lax.ppermute(sent, 'elem_2', [(0, 1), (1, 0)])]
    ppermute x1, starting transfers between devices: 1.36 us -> 2.77 us  [body(): across = lax.ppermute(sent, ELEM, list(enumerate(partner)))]
    ppermute x1, waiting for transfers between devices: 1.04 us -> 0.01 us  [body(): across = lax.ppermute(sent, ELEM, list(enumerate(partner)))]
    ppermute x1, waiting for transfers between devices: 0.01 us -> 0.42 us  [body(): within = lax.ppermute(sent, 'elem_2', [(0, 1), (1, 0)])]
    pallas_call x3 -> x2, Pallas kernels: 1.18 us -> 1.08 us  [spread(): pl.pallas_call(functools.partial(spread_kernel, groups, columns, count),...]
  transfers between devices with their start and end apart: 5 -> 5, of which waited for: 3 -> 3; matrix products, arithmetic and copies ran while one was open for 0% -> 0% of each run, Pallas kernels for 2% -> 1%
where the time goes in v4:
time: 35.2 us; the launch traced here: 35.1 us
  blocking collectives  13.9 us (39%)
  starting transfers between devices  10.6 us (30%)
  Pallas kernels  4.82 us (14%)
  waiting for transfers between devices  4.41 us (13%)
  between operations  1.32 us (4%)
    all_to_all x1, blocking collectives, body(): parts = lax.all_to_all(parts, ELEM, split_axis=0, concat_axis=0, tiled=True)  13.9 us
    ppermute x3, starting transfers between devices, body(): lax.ppermute(partial, 'grp', [(i, i ^ by) for i in range(groups)])  4.42 us
    ppermute x3, waiting for transfers between devices, body(): lax.ppermute(partial, 'grp', [(i, i ^ by) for i in range(groups)])  3.98 us
    ppermute x1, starting transfers between devices, body(): within = lax.ppermute(sent, 'elem_2', [(0, 1), (1, 0)])  3.47 us
    pallas_call x1, Pallas kernels, element_terms(): pl.pallas_call(terms_kernel, out_shape=pltpu.VMEM((SENT, LANES), jnp.floa...  2.84 us
    ppermute x1, starting transfers between devices, body(): across = lax.ppermute(sent, ELEM, list(enumerate(partner)))  2.77 us
    pallas_call x2, Pallas kernels, spread(): pl.pallas_call(functools.partial(spread_kernel, groups, columns, count),...  1.08 us
    pallas_call x1, Pallas kernels, scaled(): pl.pallas_call(functools.partial(scale_kernel, over_nodes, over_elements)...  0.72 us
  transfers between devices with their start and end apart: 5, of which 3 were waited for; matrix products, arithmetic and copies ran while one was open for 0% of the time, Pallas kernels for 1%

profile of v4, /device:TPU:1, one launch (start us, length us, event | category | flops | bytes accessed | tf_op | source)
XLA Modules:
  0.0 35.1 jit_solution(17092254045797924416)
XLA Ops:
  1.3 2.8 %shard_map.77.refs_0_ = f32[40,128]{1,0:T(8,128)S(1)} custom-call(s32[1]{0:T(128)S(6)} %copy.8.count_ref, f32[3,343,128]{2,1,0:T(8,128)} %u_hbm.1, f32[3,343,128]{2,1,0:T(8,128)} %w_hbm.1, f32[3,128]{1,0:T(4,128)} %h_hbm.1, s32[8,128]{1,0:T(8,128)} %map_hbm.1, f32[88,128]{1,0:T(8,128)} %constant.21.clone.tab_hbm), custom_call_target="tpu_custom_call" | custom-call | tf_op jit(solution)/shard_map/pallas_call | solution.py:250
  4.1 2.8 %collective-permute-start.1 = (f32[40,128]{1,0:T(8,128)S(1)}, f32[40,128]{1,0:T(8,128)S(1)}, u32[]{:S(2)}, u32[]{:S(2)}) collective-permute-start(f32[40,128]{1,0:T(8,128)S(1)} %shard_map.77.refs_0_), channel_id=1, source_target_pairs={{0,31},{1,2},{2,1},{3,4},{4,3},{5,6},{6,5},{7,8},{8,7},{9,10},{10,... | collective-permute-start | bytes 61448 | tf_op jit(solution)/shard_map/ppermute | solution.py:421
  6.9 3.5 %collective-permute-start = (f32[40,128]{1,0:T(8,128)S(1)}, f32[40,128]{1,0:T(8,128)S(1)}, u32[]{:S(2)}, u32[]{:S(2)}) collective-permute-start(f32[40,128]{1,0:T(8,128)S(1)} %shard_map.77.refs_0_), channel_id=1, source_target_pairs={{0,1},{1,0},{2,3},{3,2},{4,5},{5,4},{6,7},{7,6},{8,9},{9,8},{10,11... | collective-permute-start | bytes 61448 | tf_op jit(solution)/shard_map/ppermute | solution.py:420
  10.4 0.4 %shard_map.78.refs_2_ = f32[200,128]{1,0:T(8,128)S(1)} custom-call(s32[1]{0:T(128)} %bitcast.1.column_ref, f32[40,128]{1,0:T(8,128)S(1)} %shard_map.77.refs_0_), custom_call_target="tpu_custom_call" | custom-call | flops 100663296 | bytes 2000000 | tf_op jit(solution)/shard_map/pallas_call | solution.py:335
  10.8 0.0 collective-permute-done.1.refs_1_
  10.8 0.4 %collective-permute-done.refs_0_ = f32[40,128]{1,0:T(8,128)S(1)} collective-permute-done((f32[40,128]{1,0:T(8,128)S(1)}, f32[40,128]{1,0:T(8,128)S(1)}, u32[]{:S(2)}, u32[]{:S(2)}) %collective-permute-start) | collective-permute-done | bytes 20512 | tf_op jit(solution)/shard_map/ppermute | solution.py:420
  11.2 0.7 %shard_map.79.refs_0_ = f32[200,128]{1,0:T(8,128)S(1)} custom-call(s32[1]{0:T(128)} %bitcast.1.column_ref, f32[40,128]{1,0:T(8,128)S(1)} %collective-permute-done.refs_0_, f32[40,128]{1,0:T(8,128)S(1)} %collective-permute-done.1.refs_1_, f32[200,128]{1,0:T(8,128)S(1)} %shard_map.78.refs_2_), custom_call_target="tpu_custom_call" | custom-call | flops 201326592 | bytes 2000000 | tf_op jit(solution)/shard_map/pallas_call | solution.py:335
  11.9 3.7 %collective-permute-start.4 = (f32[200,128]{1,0:T(8,128)S(1)}, f32[200,128]{1,0:T(8,128)S(1)}, u32[]{:S(2)}, u32[]{:S(2)}) collective-permute-start(f32[200,128]{1,0:T(8,128)S(1)} %shard_map.79.refs_0_), channel_id=1, source_target_pairs={{0,64},{32,96},{64,0},{96,32},{1,65},{33,97},{65,1},{97,33},{2,66}... | collective-permute-start | bytes 307208 | tf_op jit(solution)/shard_map/ppermute | solution.py:425
  15.6 0.4 %collective-permute-start.3 = (f32[200,128]{1,0:T(8,128)S(1)}, f32[200,128]{1,0:T(8,128)S(1)}, u32[]{:S(2)}, u32[]{:S(2)}) collective-permute-start(f32[200,128]{1,0:T(8,128)S(1)} %shard_map.79.refs_0_), channel_id=1, source_target_pairs={{0,96},{32,64},{64,32},{96,0},{1,97},{33,65},{65,33},{97,1},{2,98}... | collective-permute-start | bytes 307208 | tf_op jit(solution)/shard_map/ppermute | solution.py:425
  16.0 0.3 collective-permute-start.2
  16.3 1.3 %collective-permute-done.4.refs_3_ = f32[200,128]{1,0:T(8,128)S(1)} collective-permute-done((f32[200,128]{1,0:T(8,128)S(1)}, f32[200,128]{1,0:T(8,128)S(1)}, u32[]{:S(2)}, u32[]{:S(2)}) %collective-permute-start.4) | collective-permute-done | bytes 102432 | tf_op jit(solution)/shard_map/ppermute | solution.py:425
  17.6 2.7 %collective-permute-done.3.refs_2_ = f32[200,128]{1,0:T(8,128)S(1)} collective-permute-done((f32[200,128]{1,0:T(8,128)S(1)}, f32[200,128]{1,0:T(8,128)S(1)}, u32[]{:S(2)}, u32[]{:S(2)}) %collective-permute-start.3) | collective-permute-done | bytes 102432 | tf_op jit(solution)/shard_map/ppermute | solution.py:425
  20.3 0.0 collective-permute-done.2.refs_1_
  20.3 0.2 shard_map.80
  20.5 13.9 %all_to_all.5.part_ref = f32[32,1,128]{2,1,0:T(1,128)S(1)} all-to-all(f32[32,1,128]{2,1,0:T(1,128)S(1)} %get-tuple-element.7), channel_id=1, replica_groups=mesh['grp'=4,'elem_0'=4,'elem_1'=4,'elem_2'=2] {'elem_0','elem_1','elem_2'}, dimensions={0} | all-to-all | bytes 32768 | tf_op jit(solution)/shard_map/all_to_all | solution.py:428
  34.3 0.7 %shard_map.81 = (f32[3,2048]{1,0:T(4,128)}, f32[1,1]{1,0:T(1,128)}) custom-call(f32[3,2048]{1,0:T(4,128)S(1)} %get-tuple-element.6.grad_ref, f32[32,1,128]{2,1,0:T(1,128)S(1)} %all_to_all.5.part_ref), custom_call_target="tpu_custom_call" | custom-call | tf_op jit(solution)/shard_map/pallas_call | solution.py:400
Async XLA Ops:
  4.1 6.6 %collective-permute-start.1 = (f32[40,128]{1,0:T(8,128)S(1)}, f32[40,128]{1,0:T(8,128)S(1)}, u32[]{:S(2)}, u32[]{:S(2)}) collective-permute-start(f32[40,128]{1,0:T(8,128)S(1)} %shard_map.77.refs_0_), channel_id=1, source_target_pairs={{0,31},{1,2},{2,1},{3,4},{4,3},{5,6},{6,5},{7,8},{8,7},{9,10},{10,... | collective-permute-start | bytes 61448 | tf_op jit(solution)/shard_map/ppermute | solution.py:421
  6.9 4.3 %collective-permute-start = (f32[40,128]{1,0:T(8,128)S(1)}, f32[40,128]{1,0:T(8,128)S(1)}, u32[]{:S(2)}, u32[]{:S(2)}) collective-permute-start(f32[40,128]{1,0:T(8,128)S(1)} %shard_map.77.refs_0_), channel_id=1, source_target_pairs={{0,1},{1,0},{2,3},{3,2},{4,5},{5,4},{6,7},{7,6},{8,9},{9,8},{10,11... | collective-permute-start | bytes 61448 | tf_op jit(solution)/shard_map/ppermute | solution.py:420
  11.9 5.7 %collective-permute-start.4 = (f32[200,128]{1,0:T(8,128)S(1)}, f32[200,128]{1,0:T(8,128)S(1)}, u32[]{:S(2)}, u32[]{:S(2)}) collective-permute-start(f32[200,128]{1,0:T(8,128)S(1)} %shard_map.79.refs_0_), channel_id=1, source_target_pairs={{0,64},{32,96},{64,0},{96,32},{1,65},{33,97},{65,1},{97,33},{2,66}... | collective-permute-start | bytes 307208 | tf_op jit(solution)/shard_map/ppermute | solution.py:425
  15.6 4.7 %collective-permute-start.3 = (f32[200,128]{1,0:T(8,128)S(1)}, f32[200,128]{1,0:T(8,128)S(1)}, u32[]{:S(2)}, u32[]{:S(2)}) collective-permute-start(f32[200,128]{1,0:T(8,128)S(1)} %shard_map.79.refs_0_), channel_id=1, source_target_pairs={{0,96},{32,64},{64,32},{96,0},{1,97},{33,65},{65,33},{97,1},{2,98}... | collective-permute-start | bytes 307208 | tf_op jit(solution)/shard_map/ppermute | solution.py:425
  16.0 4.3 %collective-permute-start.2 = (f32[200,128]{1,0:T(8,128)S(1)}, f32[200,128]{1,0:T(8,128)S(1)}, u32[]{:S(2)}, u32[]{:S(2)}) collective-permute-start(f32[200,128]{1,0:T(8,128)S(1)} %shard_map.79.refs_0_), channel_id=1, source_target_pairs={{0,32},{32,0},{64,96},{96,64},{1,33},{33,1},{65,97},{97,65},{2,34}... | collective-permute-start | bytes 307208 | tf_op jit(solution)/shard_map/ppermute | solution.py:425

commit v5 on v4

--- a/solution.py
+++ b/solution.py
@@ -120,7 +120,12 @@
     n = P_SIZE
     fields = [(ref, i) for ref in (u_ref, w_ref) for i in range(3)]
     rows = pl.ds(0, n)
-    pairs = [(source.at[i], ref.at[i]) for source, ref in ((u_hbm, u_ref), (w_hbm, w_ref)) for i in range(3)]
+    whole = pl.ds(0, NODES)
+    pairs = [
+        (source.at[i], ref.at[i, whole])
+        for source, ref in ((u_hbm, u_ref), (w_hbm, w_ref))
+        for i in range(3)
+    ]
     pairs += [(tab_hbm, tab_ref), (h_hbm, h_ref), (map_hbm, map_ref)]
     copies = [
         pltpu.make_async_copy(source, target, sems.at[i])
@@ -254,14 +259,14 @@
         + [pl.BlockSpec(memory_space=pltpu.HBM)] * 5,
         out_specs=vmem,
         scratch_shapes=[
-            pltpu.VMEM(velocity.shape, jnp.float32),
-            pltpu.VMEM(adjoint.shape, jnp.float32),
+            pltpu.VMEM((3, NODES + 9, LANES), jnp.float32),
+            pltpu.VMEM((3, NODES + 9, LANES), jnp.float32),
             pltpu.VMEM(spacing.shape, jnp.float32),
             pltpu.VMEM(design_map.shape, jnp.int32),
             pltpu.VMEM((TABLE_ROWS, LANES), jnp.float32),
             pltpu.VMEM((6, P_SIZE, P_SIZE, 8, LANES), jnp.float32),
             pltpu.VMEM((6, P_SIZE, 8, LANES), jnp.float32),
-            pltpu.VMEM((6 * P_SIZE * PITCH, LANES), jnp.float32),
+            pltpu.VMEM((6 * P_SIZE * PITCH + 16, LANES), jnp.float32),
             pltpu.VMEM((25, 8, LANES), jnp.float32),
             pltpu.SemaphoreType.DMA((9,)),
         ],

time: 35.2 us -> 35.2 us (level)
  no operation moved by 1% of the time
where the time goes in v5:
time: 35.2 us; the launch traced here: 35.1 us
  blocking collectives  13.9 us (39%)
  starting transfers between devices  10.6 us (30%)
  Pallas kernels  4.82 us (14%)
  waiting for transfers between devices  4.41 us (13%)
  between operations  1.32 us (4%)
    all_to_all x1, blocking collectives, body(): parts = lax.all_to_all(parts, ELEM, split_axis=0, concat_axis=0, tiled=True)  13.9 us
    ppermute x3, starting transfers between devices, body(): lax.ppermute(partial, 'grp', [(i, i ^ by) for i in range(groups)])  4.42 us
    ppermute x3, waiting for transfers between devices, body(): lax.ppermute(partial, 'grp', [(i, i ^ by) for i in range(groups)])  3.98 us
    ppermute x1, starting transfers between devices, body(): within = lax.ppermute(sent, 'elem_2', [(0, 1), (1, 0)])  3.47 us
    pallas_call x1, Pallas kernels, element_terms(): pl.pallas_call(terms_kernel, out_shape=pltpu.VMEM((SENT, LANES), jnp.floa...  2.84 us
    ppermute x1, starting transfers between devices, body(): across = lax.ppermute(sent, ELEM, list(enumerate(partner)))  2.77 us
    pallas_call x2, Pallas kernels, spread(): pl.pallas_call(functools.partial(spread_kernel, groups, columns, count),...  1.08 us
    pallas_call x1, Pallas kernels, scaled(): pl.pallas_call(functools.partial(scale_kernel, over_nodes, over_elements)...  0.72 us
  transfers between devices with their start and end apart: 5, of which 3 were waited for; matrix products, arithmetic and copies ran while one was open for 0% of the time, Pallas kernels for 1%

profile of v5, /device:TPU:1, one launch (start us, length us, event | category | flops | bytes accessed | tf_op | source)
XLA Modules:
  0.0 35.1 jit_solution(9845340035785126805)
XLA Ops:
  1.3 2.8 %shard_map.77.refs_0_ = f32[40,128]{1,0:T(8,128)S(1)} custom-call(s32[1]{0:T(128)S(6)} %copy.8.count_ref, f32[3,343,128]{2,1,0:T(8,128)} %u_hbm.1, f32[3,343,128]{2,1,0:T(8,128)} %w_hbm.1, f32[3,128]{1,0:T(4,128)} %h_hbm.1, s32[8,128]{1,0:T(8,128)} %map_hbm.1, f32[88,128]{1,0:T(8,128)} %constant.21.clone.tab_hbm), custom_call_target="tpu_custom_call" | custom-call | tf_op jit(solution)/shard_map/pallas_call | solution.py:255
  4.1 2.8 %collective-permute-start.1 = (f32[40,128]{1,0:T(8,128)S(1)}, f32[40,128]{1,0:T(8,128)S(1)}, u32[]{:S(2)}, u32[]{:S(2)}) collective-permute-start(f32[40,128]{1,0:T(8,128)S(1)} %shard_map.77.refs_0_), channel_id=1, source_target_pairs={{0,31},{1,2},{2,1},{3,4},{4,3},{5,6},{6,5},{7,8},{8,7},{9,10},{10,... | collective-permute-start | bytes 61448 | tf_op jit(solution)/shard_map/ppermute | solution.py:426
  6.9 3.5 %collective-permute-start = (f32[40,128]{1,0:T(8,128)S(1)}, f32[40,128]{1,0:T(8,128)S(1)}, u32[]{:S(2)}, u32[]{:S(2)}) collective-permute-start(f32[40,128]{1,0:T(8,128)S(1)} %shard_map.77.refs_0_), channel_id=1, source_target_pairs={{0,1},{1,0},{2,3},{3,2},{4,5},{5,4},{6,7},{7,6},{8,9},{9,8},{10,11... | collective-permute-start | bytes 61448 | tf_op jit(solution)/shard_map/ppermute | solution.py:425
  10.4 0.4 %shard_map.78.refs_2_ = f32[200,128]{1,0:T(8,128)S(1)} custom-call(s32[1]{0:T(128)} %bitcast.1.column_ref, f32[40,128]{1,0:T(8,128)S(1)} %shard_map.77.refs_0_), custom_call_target="tpu_custom_call" | custom-call | flops 100663296 | bytes 2000000 | tf_op jit(solution)/shard_map/pallas_call | solution.py:340
  10.8 0.0 collective-permute-done.1.refs_1_
  10.8 0.4 %collective-permute-done.refs_0_ = f32[40,128]{1,0:T(8,128)S(1)} collective-permute-done((f32[40,128]{1,0:T(8,128)S(1)}, f32[40,128]{1,0:T(8,128)S(1)}, u32[]{:S(2)}, u32[]{:S(2)}) %collective-permute-start) | collective-permute-done | bytes 20512 | tf_op jit(solution)/shard_map/ppermute | solution.py:425
  11.2 0.7 %shard_map.79.refs_0_ = f32[200,128]{1,0:T(8,128)S(1)} custom-call(s32[1]{0:T(128)} %bitcast.1.column_ref, f32[40,128]{1,0:T(8,128)S(1)} %collective-permute-done.refs_0_, f32[40,128]{1,0:T(8,128)S(1)} %collective-permute-done.1.refs_1_, f32[200,128]{1,0:T(8,128)S(1)} %shard_map.78.refs_2_), custom_call_target="tpu_custom_call" | custom-call | flops 201326592 | bytes 2000000 | tf_op jit(solution)/shard_map/pallas_call | solution.py:340
  11.9 3.7 %collective-permute-start.4 = (f32[200,128]{1,0:T(8,128)S(1)}, f32[200,128]{1,0:T(8,128)S(1)}, u32[]{:S(2)}, u32[]{:S(2)}) collective-permute-start(f32[200,128]{1,0:T(8,128)S(1)} %shard_map.79.refs_0_), channel_id=1, source_target_pairs={{0,64},{32,96},{64,0},{96,32},{1,65},{33,97},{65,1},{97,33},{2,66}... | collective-permute-start | bytes 307208 | tf_op jit(solution)/shard_map/ppermute | solution.py:430
  15.6 0.4 %collective-permute-start.3 = (f32[200,128]{1,0:T(8,128)S(1)}, f32[200,128]{1,0:T(8,128)S(1)}, u32[]{:S(2)}, u32[]{:S(2)}) collective-permute-start(f32[200,128]{1,0:T(8,128)S(1)} %shard_map.79.refs_0_), channel_id=1, source_target_pairs={{0,96},{32,64},{64,32},{96,0},{1,97},{33,65},{65,33},{97,1},{2,98}... | collective-permute-start | bytes 307208 | tf_op jit(solution)/shard_map/ppermute | solution.py:430
  16.0 0.3 collective-permute-start.2
  16.3 1.3 %collective-permute-done.4.refs_3_ = f32[200,128]{1,0:T(8,128)S(1)} collective-permute-done((f32[200,128]{1,0:T(8,128)S(1)}, f32[200,128]{1,0:T(8,128)S(1)}, u32[]{:S(2)}, u32[]{:S(2)}) %collective-permute-start.4) | collective-permute-done | bytes 102432 | tf_op jit(solution)/shard_map/ppermute | solution.py:430
  17.6 2.7 %collective-permute-done.3.refs_2_ = f32[200,128]{1,0:T(8,128)S(1)} collective-permute-done((f32[200,128]{1,0:T(8,128)S(1)}, f32[200,128]{1,0:T(8,128)S(1)}, u32[]{:S(2)}, u32[]{:S(2)}) %collective-permute-start.3) | collective-permute-done | bytes 102432 | tf_op jit(solution)/shard_map/ppermute | solution.py:430
  20.3 0.0 collective-permute-done.2.refs_1_
  20.3 0.2 shard_map.80
  20.5 13.9 %all_to_all.5.part_ref = f32[32,1,128]{2,1,0:T(1,128)S(1)} all-to-all(f32[32,1,128]{2,1,0:T(1,128)S(1)} %get-tuple-element.7), channel_id=1, replica_groups=mesh['grp'=4,'elem_0'=4,'elem_1'=4,'elem_2'=2] {'elem_0','elem_1','elem_2'}, dimensions={0} | all-to-all | bytes 32768 | tf_op jit(solution)/shard_map/all_to_all | solution.py:433
  34.3 0.7 %shard_map.81 = (f32[3,2048]{1,0:T(4,128)}, f32[1,1]{1,0:T(1,128)}) custom-call(f32[3,2048]{1,0:T(4,128)S(1)} %get-tuple-element.6.grad_ref, f32[32,1,128]{2,1,0:T(1,128)S(1)} %all_to_all.5.part_ref), custom_call_target="tpu_custom_call" | custom-call | tf_op jit(solution)/shard_map/pallas_call | solution.py:405
Async XLA Ops:
  4.1 6.6 %collective-permute-start.1 = (f32[40,128]{1,0:T(8,128)S(1)}, f32[40,128]{1,0:T(8,128)S(1)}, u32[]{:S(2)}, u32[]{:S(2)}) collective-permute-start(f32[40,128]{1,0:T(8,128)S(1)} %shard_map.77.refs_0_), channel_id=1, source_target_pairs={{0,31},{1,2},{2,1},{3,4},{4,3},{5,6},{6,5},{7,8},{8,7},{9,10},{10,... | collective-permute-start | bytes 61448 | tf_op jit(solution)/shard_map/ppermute | solution.py:426
  6.9 4.3 %collective-permute-start = (f32[40,128]{1,0:T(8,128)S(1)}, f32[40,128]{1,0:T(8,128)S(1)}, u32[]{:S(2)}, u32[]{:S(2)}) collective-permute-start(f32[40,128]{1,0:T(8,128)S(1)} %shard_map.77.refs_0_), channel_id=1, source_target_pairs={{0,1},{1,0},{2,3},{3,2},{4,5},{5,4},{6,7},{7,6},{8,9},{9,8},{10,11... | collective-permute-start | bytes 61448 | tf_op jit(solution)/shard_map/ppermute | solution.py:425
  11.9 5.7 %collective-permute-start.4 = (f32[200,128]{1,0:T(8,128)S(1)}, f32[200,128]{1,0:T(8,128)S(1)}, u32[]{:S(2)}, u32[]{:S(2)}) collective-permute-start(f32[200,128]{1,0:T(8,128)S(1)} %shard_map.79.refs_0_), channel_id=1, source_target_pairs={{0,64},{32,96},{64,0},{96,32},{1,65},{33,97},{65,1},{97,33},{2,66}... | collective-permute-start | bytes 307208 | tf_op jit(solution)/shard_map/ppermute | solution.py:430
  15.6 4.7 %collective-permute-start.3 = (f32[200,128]{1,0:T(8,128)S(1)}, f32[200,128]{1,0:T(8,128)S(1)}, u32[]{:S(2)}, u32[]{:S(2)}) collective-permute-start(f32[200,128]{1,0:T(8,128)S(1)} %shard_map.79.refs_0_), channel_id=1, source_target_pairs={{0,96},{32,64},{64,32},{96,0},{1,97},{33,65},{65,33},{97,1},{2,98}... | collective-permute-start | bytes 307208 | tf_op jit(solution)/shard_map/ppermute | solution.py:430
  16.0 4.3 %collective-permute-start.2 = (f32[200,128]{1,0:T(8,128)S(1)}, f32[200,128]{1,0:T(8,128)S(1)}, u32[]{:S(2)}, u32[]{:S(2)}) collective-permute-start(f32[200,128]{1,0:T(8,128)S(1)} %shard_map.79.refs_0_), channel_id=1, source_target_pairs={{0,32},{32,0},{64,96},{96,64},{1,33},{33,1},{65,97},{97,65},{2,34}... | collective-permute-start | bytes 307208 | tf_op jit(solution)/shard_map/ppermute | solution.py:430

commit v6 on v5

--- a/solution.py
+++ b/solution.py
@@ -17,7 +17,7 @@
 GRP_ELEM = ("grp", "elem_0", "elem_1", "elem_2")
 SENT = 40
 WIDE = 128
-UNROLL = 1
+UNROLL = 7
 PITCH = 9
 
 

time: 35.2 us -> 35.1 us (level)
  no operation moved by 1% of the time
where the time goes in v6:
time: 35.1 us; the launch traced here: 34.9 us
  blocking collectives  13.9 us (40%)
  starting transfers between devices  10.7 us (30%)
  Pallas kernels  4.71 us (13%)
  waiting for transfers between devices  4.41 us (13%)
  between operations  1.32 us (4%)
    all_to_all x1, blocking collectives, body(): parts = lax.all_to_all(parts, ELEM, split_axis=0, concat_axis=0, tiled=True)  13.9 us
    ppermute x3, starting transfers between devices, body(): lax.ppermute(partial, 'grp', [(i, i ^ by) for i in range(groups)])  4.42 us
    ppermute x3, waiting for transfers between devices, body(): lax.ppermute(partial, 'grp', [(i, i ^ by) for i in range(groups)])  3.98 us
    ppermute x1, starting transfers between devices, body(): within = lax.ppermute(sent, 'elem_2', [(0, 1), (1, 0)])  3.47 us
    ppermute x1, starting transfers between devices, body(): across = lax.ppermute(sent, ELEM, list(enumerate(partner)))  2.77 us
    pallas_call x1, Pallas kernels, element_terms(): pl.pallas_call(terms_kernel, out_shape=pltpu.VMEM((SENT, LANES), jnp.floa...  2.74 us
    pallas_call x2, Pallas kernels, spread(): pl.pallas_call(functools.partial(spread_kernel, groups, columns, count),...  1.08 us
    pallas_call x1, Pallas kernels, scaled(): pl.pallas_call(functools.partial(scale_kernel, over_nodes, over_elements)...  0.72 us
  transfers between devices with their start and end apart: 5, of which 3 were waited for; matrix products, arithmetic and copies ran while one was open for 0% of the time, Pallas kernels for 1%

profile of v6, /device:TPU:1, one launch (start us, length us, event | category | flops | bytes accessed | tf_op | source)
XLA Modules:
  0.0 34.9 jit_solution(2817859797992036575)
XLA Ops:
  1.3 2.7 %shard_map.77.refs_0_ = f32[40,128]{1,0:T(8,128)S(1)} custom-call(s32[1]{0:T(128)S(6)} %copy.8.count_ref, f32[3,343,128]{2,1,0:T(8,128)} %u_hbm.1, f32[3,343,128]{2,1,0:T(8,128)} %w_hbm.1, f32[3,128]{1,0:T(4,128)} %h_hbm.1, s32[8,128]{1,0:T(8,128)} %map_hbm.1, f32[88,128]{1,0:T(8,128)} %constant.21.clone.tab_hbm), custom_call_target="tpu_custom_call" | custom-call | tf_op jit(solution)/shard_map/pallas_call | solution.py:255
  4.0 2.8 %collective-permute-start.1 = (f32[40,128]{1,0:T(8,128)S(1)}, f32[40,128]{1,0:T(8,128)S(1)}, u32[]{:S(2)}, u32[]{:S(2)}) collective-permute-start(f32[40,128]{1,0:T(8,128)S(1)} %shard_map.77.refs_0_), channel_id=1, source_target_pairs={{0,31},{1,2},{2,1},{3,4},{4,3},{5,6},{6,5},{7,8},{8,7},{9,10},{10,... | collective-permute-start | bytes 61448 | tf_op jit(solution)/shard_map/ppermute | solution.py:426
  6.8 3.5 %collective-permute-start = (f32[40,128]{1,0:T(8,128)S(1)}, f32[40,128]{1,0:T(8,128)S(1)}, u32[]{:S(2)}, u32[]{:S(2)}) collective-permute-start(f32[40,128]{1,0:T(8,128)S(1)} %shard_map.77.refs_0_), channel_id=1, source_target_pairs={{0,1},{1,0},{2,3},{3,2},{4,5},{5,4},{6,7},{7,6},{8,9},{9,8},{10,11... | collective-permute-start | bytes 61448 | tf_op jit(solution)/shard_map/ppermute | solution.py:425
  10.3 0.4 %shard_map.78.refs_2_ = f32[200,128]{1,0:T(8,128)S(1)} custom-call(s32[1]{0:T(128)} %bitcast.1.column_ref, f32[40,128]{1,0:T(8,128)S(1)} %shard_map.77.refs_0_), custom_call_target="tpu_custom_call" | custom-call | flops 100663296 | bytes 2000000 | tf_op jit(solution)/shard_map/pallas_call | solution.py:340
  10.7 0.0 collective-permute-done.1.refs_1_
  10.7 0.4 %collective-permute-done.refs_0_ = f32[40,128]{1,0:T(8,128)S(1)} collective-permute-done((f32[40,128]{1,0:T(8,128)S(1)}, f32[40,128]{1,0:T(8,128)S(1)}, u32[]{:S(2)}, u32[]{:S(2)}) %collective-permute-start) | collective-permute-done | bytes 20512 | tf_op jit(solution)/shard_map/ppermute | solution.py:425
  11.1 0.7 %shard_map.79.refs_0_ = f32[200,128]{1,0:T(8,128)S(1)} custom-call(s32[1]{0:T(128)} %bitcast.1.column_ref, f32[40,128]{1,0:T(8,128)S(1)} %collective-permute-done.refs_0_, f32[40,128]{1,0:T(8,128)S(1)} %collective-permute-done.1.refs_1_, f32[200,128]{1,0:T(8,128)S(1)} %shard_map.78.refs_2_), custom_call_target="tpu_custom_call" | custom-call | flops 201326592 | bytes 2000000 | tf_op jit(solution)/shard_map/pallas_call | solution.py:340
  11.8 3.7 %collective-permute-start.4 = (f32[200,128]{1,0:T(8,128)S(1)}, f32[200,128]{1,0:T(8,128)S(1)}, u32[]{:S(2)}, u32[]{:S(2)}) collective-permute-start(f32[200,128]{1,0:T(8,128)S(1)} %shard_map.79.refs_0_), channel_id=1, source_target_pairs={{0,64},{32,96},{64,0},{96,32},{1,65},{33,97},{65,1},{97,33},{2,66}... | collective-permute-start | bytes 307208 | tf_op jit(solution)/shard_map/ppermute | solution.py:430
  15.5 0.4 %collective-permute-start.3 = (f32[200,128]{1,0:T(8,128)S(1)}, f32[200,128]{1,0:T(8,128)S(1)}, u32[]{:S(2)}, u32[]{:S(2)}) collective-permute-start(f32[200,128]{1,0:T(8,128)S(1)} %shard_map.79.refs_0_), channel_id=1, source_target_pairs={{0,96},{32,64},{64,32},{96,0},{1,97},{33,65},{65,33},{97,1},{2,98}... | collective-permute-start | bytes 307208 | tf_op jit(solution)/shard_map/ppermute | solution.py:430
  15.9 0.3 collective-permute-start.2
  16.2 1.3 %collective-permute-done.4.refs_3_ = f32[200,128]{1,0:T(8,128)S(1)} collective-permute-done((f32[200,128]{1,0:T(8,128)S(1)}, f32[200,128]{1,0:T(8,128)S(1)}, u32[]{:S(2)}, u32[]{:S(2)}) %collective-permute-start.4) | collective-permute-done | bytes 102432 | tf_op jit(solution)/shard_map/ppermute | solution.py:430
  17.5 2.7 %collective-permute-done.3.refs_2_ = f32[200,128]{1,0:T(8,128)S(1)} collective-permute-done((f32[200,128]{1,0:T(8,128)S(1)}, f32[200,128]{1,0:T(8,128)S(1)}, u32[]{:S(2)}, u32[]{:S(2)}) %collective-permute-start.3) | collective-permute-done | bytes 102432 | tf_op jit(solution)/shard_map/ppermute | solution.py:430
  20.2 0.0 collective-permute-done.2.refs_1_
  20.2 0.2 shard_map.80
  20.4 13.9 %all_to_all.5.part_ref = f32[32,1,128]{2,1,0:T(1,128)S(1)} all-to-all(f32[32,1,128]{2,1,0:T(1,128)S(1)} %get-tuple-element.7), channel_id=1, replica_groups=mesh['grp'=4,'elem_0'=4,'elem_1'=4,'elem_2'=2] {'elem_0','elem_1','elem_2'}, dimensions={0} | all-to-all | bytes 32768 | tf_op jit(solution)/shard_map/all_to_all | solution.py:433
  34.2 0.7 %shard_map.81 = (f32[3,2048]{1,0:T(4,128)}, f32[1,1]{1,0:T(1,128)}) custom-call(f32[3,2048]{1,0:T(4,128)S(1)} %get-tuple-element.6.grad_ref, f32[32,1,128]{2,1,0:T(1,128)S(1)} %all_to_all.5.part_ref), custom_call_target="tpu_custom_call" | custom-call | tf_op jit(solution)/shard_map/pallas_call | solution.py:405
Async XLA Ops:
  4.0 6.6 %collective-permute-start.1 = (f32[40,128]{1,0:T(8,128)S(1)}, f32[40,128]{1,0:T(8,128)S(1)}, u32[]{:S(2)}, u32[]{:S(2)}) collective-permute-start(f32[40,128]{1,0:T(8,128)S(1)} %shard_map.77.refs_0_), channel_id=1, source_target_pairs={{0,31},{1,2},{2,1},{3,4},{4,3},{5,6},{6,5},{7,8},{8,7},{9,10},{10,... | collective-permute-start | bytes 61448 | tf_op jit(solution)/shard_map/ppermute | solution.py:426
  6.8 4.3 %collective-permute-start = (f32[40,128]{1,0:T(8,128)S(1)}, f32[40,128]{1,0:T(8,128)S(1)}, u32[]{:S(2)}, u32[]{:S(2)}) collective-permute-start(f32[40,128]{1,0:T(8,128)S(1)} %shard_map.77.refs_0_), channel_id=1, source_target_pairs={{0,1},{1,0},{2,3},{3,2},{4,5},{5,4},{6,7},{7,6},{8,9},{9,8},{10,11... | collective-permute-start | bytes 61448 | tf_op jit(solution)/shard_map/ppermute | solution.py:425
  11.8 5.7 %collective-permute-start.4 = (f32[200,128]{1,0:T(8,128)S(1)}, f32[200,128]{1,0:T(8,128)S(1)}, u32[]{:S(2)}, u32[]{:S(2)}) collective-permute-start(f32[200,128]{1,0:T(8,128)S(1)} %shard_map.79.refs_0_), channel_id=1, source_target_pairs={{0,64},{32,96},{64,0},{96,32},{1,65},{33,97},{65,1},{97,33},{2,66}... | collective-permute-start | bytes 307208 | tf_op jit(solution)/shard_map/ppermute | solution.py:430
  15.5 4.7 %collective-permute-start.3 = (f32[200,128]{1,0:T(8,128)S(1)}, f32[200,128]{1,0:T(8,128)S(1)}, u32[]{:S(2)}, u32[]{:S(2)}) collective-permute-start(f32[200,128]{1,0:T(8,128)S(1)} %shard_map.79.refs_0_), channel_id=1, source_target_pairs={{0,96},{32,64},{64,32},{96,0},{1,97},{33,65},{65,33},{97,1},{2,98}... | collective-permute-start | bytes 307208 | tf_op jit(solution)/shard_map/ppermute | solution.py:430
  15.9 4.3 %collective-permute-start.2 = (f32[200,128]{1,0:T(8,128)S(1)}, f32[200,128]{1,0:T(8,128)S(1)}, u32[]{:S(2)}, u32[]{:S(2)}) collective-permute-start(f32[200,128]{1,0:T(8,128)S(1)} %shard_map.79.refs_0_), channel_id=1, source_target_pairs={{0,32},{32,0},{64,96},{96,64},{1,33},{33,1},{65,97},{97,65},{2,34}... | collective-permute-start | bytes 307208 | tf_op jit(solution)/shard_map/ppermute | solution.py:430
